TPU v7x, 32 devices: a whole 2x2x4 slice. The times are simulated.
32 devices in a mesh: chain: 8 (over y, x, core), sector: 4 (over z).
Axes of the slice: x: 2, y: 2, z: 4, core: 2. Of those that a mesh axis runs over, the one named last changes fastest.
Arguments:
- psi: float32 [8, 16, 256, 256], P('chain', 'sector'), may hold values from -6 to 6
- kept_rank: int32 [8, 16], P('chain', 'sector'), may hold values from 64 to 256, as said below
- step_size: float32 [8, 3], P('chain'), may hold values from 0.2 to 0.6
- left_env: bfloat16 [8, 2, 16, 256, 256], P('chain', None, 'sector'), may hold values from -0.375 to 0.375
- right_env: bfloat16 [8, 2, 16, 256, 256], P('chain', None, 'sector'), may hold values from -0.375 to 0.375
- hop_left: bfloat16 [8, 2, 16, 256, 256], P('chain', None, 'sector'), may hold values from -0.375 to 0.375
- hop_right: bfloat16 [8, 2, 16, 256, 256], P('chain', None, 'sector'), may hold values from -0.375 to 0.375
- hop_source: int32 [2, 16], replicated, may hold values from 0 to 15, each once within a row
Outputs:
- site_state: float32 [8, 16, 256, 256], P('chain', 'sector')
- merged_left: float32 [8, 2, 16, 256, 256], P('chain', None, 'sector')
- merged_right: float32 [8, 2, 16, 256, 256], P('chain', None, 'sector')
Inputs may be any that keep to these rules, and one draw needn't show every extreme that they name: `kept_rank`: each partition has one sector whose kept rank is the full 256.
All inputs are finite; a program needn't handle non-finite values.
Results may differ from a plain program's by a relative error of at most 0.009.
Values may be sent and summed in bfloat16 or wider, within the bound.
No kernel may reach another device: no remote copies, remote signals or barrier semaphores. Data moves between devices by JAX's collectives and lax.ppermute only.
A program may use at most 64 MiB of HBM per device.

v0:
```python
import jax
import jax.numpy as jnp
from jax import lax
from jax.sharding import PartitionSpec as P

STEPS = 3


def from_behind(value, axis, steps):
    count = lax.axis_size(axis)
    initial, last = (max(0, -steps), min(count, count - steps))
    return lax.ppermute(value, axis, [(source, source + steps) for source in range(initial, last)])


def on_device(psi, kept_rank, step_size, left_env, right_env, hop_left, hop_right, hop_source):
    f32 = jnp.float32
    bf16 = jnp.bfloat16
    sec_count = psi.shape[1]
    block_size = psi.shape[2]
    chi_total = sec_count * lax.axis_size("sector") * block_size
    first_sector = lax.axis_index("sector") * sec_count
    sources = lax.dynamic_slice_in_dim(hop_source, first_sector, sec_count, 1)
    row_index = lax.broadcasted_iota(jnp.int32, (sec_count, block_size), 1)
    kept_rows = (row_index < kept_rank[0][:, None]).astype(f32)
    mask = kept_rows[:, :, None] * kept_rows[:, None, :]
    left_one = left_env[0]
    right_one = right_env[0]
    hop_first = hop_left[0]
    hop_second = hop_right[0]
    state = psi[0] * mask
    for step in range(STEPS):
        state_b = state.astype(bf16)
        inner = jnp.einsum("atij,tjk->atik", left_one, state_b, preferred_element_type=f32).astype(
            bf16
        )
        image = jnp.einsum("atik,atkl->til", inner, right_one, preferred_element_type=f32)
        gathered = lax.all_gather(state_b, "sector", axis=0, tiled=True)
        picked = gathered[sources]
        hop_inner = jnp.einsum(
            "btij,btjk->btik", hop_first, picked, preferred_element_type=f32
        ).astype(bf16)
        image = (
            image + jnp.einsum("btik,btkl->til", hop_inner, hop_second, preferred_element_type=f32)
        ) * mask
        step_now = step_size[0, step]
        self_dot, cross, image_dot = lax.psum(
            (jnp.sum(state * state), jnp.sum(state * image), jnp.sum(image * image)), "sector"
        )
        quotient = cross / self_dot
        state_resid = cross - quotient * self_dot
        resid_dot = image_dot - 2.0 * quotient * cross + quotient * quotient * self_dot
        new_dot = self_dot - 2.0 * step_now * state_resid + step_now * step_now * resid_dot
        state = state - step_now * (image - quotient * state)
        state = state / jnp.sqrt(new_dot)
    final_b = state.astype(bf16)
    left_half = jnp.einsum("tji,atjk->atik", final_b, left_one, preferred_element_type=f32).astype(
        bf16
    )
    right_half = jnp.einsum(
        "atij,tkj->atik", right_one, final_b, preferred_element_type=f32
    ).astype(bf16)
    left_own = chi_total * jnp.einsum(
        "atik,tkl->atil", left_half, final_b, preferred_element_type=f32
    )
    right_own = chi_total * jnp.einsum(
        "tij,atjk->atik", final_b, right_half, preferred_element_type=f32
    )
    left_new = from_behind(left_own.astype(jnp.bfloat16), "chain", 1).astype(left_own.dtype)
    right_new = from_behind(right_own.astype(jnp.bfloat16), "chain", -1).astype(right_own.dtype)
    merged_left = left_one.astype(f32) + left_new
    merged_right = right_one.astype(f32) + right_new
    return (state[None], merged_left[None], merged_right[None])


def solution(mesh):
    placed = (
        P("chain", "sector", None, None),
        P("chain", "sector"),
        P("chain", None),
        P("chain", None, "sector", None, None),
        P("chain", None, "sector", None, None),
        P("chain", None, "sector", None, None),
        P("chain", None, "sector", None, None),
        P(),
    )
    return jax.shard_map(
        on_device,
        mesh=mesh,
        in_specs=placed,
        out_specs=(
            P("chain", "sector", None, None),
            P("chain", None, "sector", None, None),
            P("chain", None, "sector", None, None),
        ),
        check_vma=False,
    )
```

profile of v0, /device:TPU:1, one launch (start us, length us, event | category | flops | bytes accessed | tf_op | source)
XLA Modules:
  0.0 276.3 jit_solution(8332894562463598212)
XLA Ops:
  7.2 0.0 copy-start
  7.2 0.0 copy-start.7
  7.2 0.0 copy-start.6
  7.2 0.0 copy-start.5
  7.2 0.0 all-gather.4.cloned.1.call-start
  7.3 0.9 fusion.59
  8.1 2.2 fusion.44
  10.3 0.0 all-gather.4.cloned.1.call-update
  10.4 0.0 all-gather.6.cloned.1.call-start
  10.4 0.0 copy-done.7
  10.4 0.1 compare_select_fusion
  10.5 0.1 reshape.49
  10.6 0.0 copy-done.6
  10.6 0.7 fusion.62
  12.9 0.0 copy-done.5
  12.9 0.5 copy.22
  13.5 1.5 copy.34
  15.0 0.0 copy-start.2
  15.0 43.5 %all-gather.4.cloned.1.call-done = bf16[16,256,256]{2,1,0:T(8,128)(2,1)} async-done(((bf16[4,256,256]{2,1,0:T(8,128)(2,1)}), bf16[16,256,256]{2,1,0:T(8,128)(2,1)}) %all-gather.4.cloned.1.call-update) | async-done | bytes 2097168 | tf_op jit(solution)/shard_map/all_gather | solution.py:37
  58.5 3.2 %gather_fusion = bf16[8,256,256]{2,1,0:T(8,128)(2,1)} fusion(bf16[16,256,256]{2,1,0:T(8,128)(2,1)} %all-gather.4.cloned.1.call-done, s32[1024]{0:T(1024)S(1)} %pad_clamp_fusion), kind=kCustom, calls=%fused_computation | custom fusion | bytes 2097184 | tf_op jit(solution)/shard_map/gather | solution.py:38
  61.7 0.0 copy-done
  61.7 3.2 %fusion.2 = f32[4,256,256]{2,1,0:T(8,128)} fusion(bf16[2,4,256,256]{3,2,1,0:T(8,128)(2,1)} %bitcast.198, bf16[1,2,4,256,256]{4,3,2,1,0:T(8,128)(2,1)S(1)} %copy-done, bf16[1,2,4,256,256]{4,3,2,1,0:T(8,128)(2,1)} %param.13), kind=kOutput, calls=%fused_computation.21 | convolution fusion | flops 537395200 | bytes 4194304 | tf_op jit(solution)/shard_map/btik,btkl->til/dot_general | solution.py:43
  64.9 0.0 copy-done.2
  64.9 4.8 %multiply_reduce_fusion.8 = (f32[]{:T(128)}, f32[]{:T(128)}, f32[]{:T(128)}, f32[4,256,256]{2,1,0:T(8,128)}) fusion(f32[1,4,256,256]{3,2,1,0:T(8,128)} %param.8, f32[4,256]{1,0:T(4,128)S(1)} %fusion.59, f32[4,256,256]{2,1,0:T(8,128)} %fusion.2, bf16[2,4,256,256]{2,3,0,1:T(8,128)(2,1)S(1)} %copy.34, bf16[1,2,4,256,256]{3,4,1,2,0:T(8,128)(2,1)S(1)} %copy.22), kind=kOutput, calls=%fused_computation.60 | convolution fusion | flops 540803072 | bytes 5246988 | tf_op jit(solution)/shard_map/atik,atkl->til/dot_general | solution.py:36
  69.8 8.4 %all-reduce.2 = (f32[]{:T(128)}, f32[]{:T(128)}, f32[]{:T(128)}) all-reduce(f32[]{:T(128)} %get-tuple-element.10, f32[]{:T(128)} %get-tuple-element.9, f32[]{:T(128)} %get-tuple-element.17), channel_id=1, replica_groups=mesh['chain'=8,'sector'=4] {'sector'}, use_global_device_ids=true, to_apply=%region_3.0 | all-reduce | flops 3 | bytes 24 | tf_op jit(solution)/shard_map/psum | solution.py:46
  83.3 3.2 %fusion.61 = (bf16[4,256,256]{2,1,0:T(8,128)(2,1)}, f32[4,256,256]{2,1,0:T(8,128)S(1)}) fusion(f32[]{:T(128)S(6)} %sqrt.9, f32[4,256,256]{2,1,0:T(8,128)} %get-tuple-element.34, f32[]{:T(128)S(6)} %div.27, f32[]{:T(128)} %bitcast.2, f32[4,256]{1,0:T(4,128)S(1)} %fusion.59, f32[1,4,256,256]{3,2,1,0:T(8,128)} %param.8), kind=kLoop, calls=%fused_computation.80 | loop fusion | flops 2097152 | bytes 3674124 | tf_op jit(solution)/shard_map/convert_element_type | solution.py:32
  86.6 0.0 all-gather.6.cloned.1.call-update
  86.6 0.0 all-gather.8.cloned.1.call-start
  88.5 44.4 %all-gather.6.cloned.1.call-done = bf16[16,256,256]{2,1,0:T(8,128)(2,1)} async-done(((bf16[4,256,256]{2,1,0:T(8,128)(2,1)}), bf16[16,256,256]{2,1,0:T(8,128)(2,1)}) %all-gather.6.cloned.1.call-update) | async-done | bytes 2097168 | tf_op jit(solution)/shard_map/all_gather | solution.py:37
  132.9 3.2 %gather_fusion.1 = bf16[8,256,256]{2,1,0:T(8,128)(2,1)} fusion(bf16[16,256,256]{2,1,0:T(8,128)(2,1)} %all-gather.6.cloned.1.call-done, s32[1024]{0:T(1024)S(1)} %pad_clamp_fusion), kind=kCustom, calls=%fused_computation.1 | custom fusion | bytes 2097184 | tf_op jit(solution)/shard_map/gather | solution.py:38
  136.1 3.2 %fusion.5 = f32[4,256,256]{2,1,0:T(8,128)} fusion(bf16[2,4,256,256]{3,2,1,0:T(8,128)(2,1)} %bitcast.199, bf16[1,2,4,256,256]{4,3,2,1,0:T(8,128)(2,1)S(1)} %copy-done, bf16[1,2,4,256,256]{4,3,2,1,0:T(8,128)(2,1)} %param.13), kind=kOutput, calls=%fused_computation.24 | convolution fusion | flops 537395200 | bytes 4194304 | tf_op jit(solution)/shard_map/btik,btkl->til/dot_general | solution.py:43
  139.3 4.2 %multiply_reduce_fusion.3 = (f32[]{:T(128)}, f32[]{:T(128)}, f32[]{:T(128)}, f32[4,256,256]{2,1,0:T(8,128)}) fusion(f32[4,256,256]{2,1,0:T(8,128)S(1)} %get-tuple-element.30, f32[4,256]{1,0:T(4,128)S(1)} %fusion.59, f32[4,256,256]{2,1,0:T(8,128)} %fusion.5, bf16[2,4,256,256]{2,3,0,1:T(8,128)(2,1)} %copy-done.2, bf16[1,2,4,256,256]{3,4,1,2,0:T(8,128)(2,1)S(1)} %copy.22, ...), kind=kOutput, calls=%fused_computation.53 | convolution fusion | flops 539754496 | bytes 5771276 | tf_op jit(solution)/shard_map/atik,atkl->til/dot_general | solution.py:36
  143.5 8.4 %all-reduce.1 = (f32[]{:T(128)}, f32[]{:T(128)}, f32[]{:T(128)}) all-reduce(f32[]{:T(128)} %get-tuple-element.16, f32[]{:T(128)} %get-tuple-element.15, f32[]{:T(128)} %get-tuple-element.14), channel_id=1, replica_groups=mesh['chain'=8,'sector'=4] {'sector'}, use_global_device_ids=true, to_apply=%region_9.0 | all-reduce | flops 3 | bytes 24 | tf_op jit(solution)/shard_map/psum | solution.py:46
  157.1 3.2 %fusion.60 = (bf16[4,256,256]{2,1,0:T(8,128)(2,1)}, f32[4,256,256]{2,1,0:T(8,128)}) fusion(f32[]{:T(128)S(6)} %sqrt.10, f32[4,256,256]{2,1,0:T(8,128)S(1)} %get-tuple-element.30, f32[4,256,256]{2,1,0:T(8,128)} %get-tuple-element.35, f32[]{:T(128)S(6)} %div.30, f32[]{:T(128)} %bitcast.17), kind=kLoop, calls=%fused_computation.79 | loop fusion | flops 1572864 | bytes 3670028 | tf_op jit(solution)/shard_map/convert_element_type | solution.py:32
  160.3 0.0 all-gather.8.cloned.1.call-update
  162.2 44.5 %all-gather.8.cloned.1.call-done = bf16[16,256,256]{2,1,0:T(8,128)(2,1)} async-done(((bf16[4,256,256]{2,1,0:T(8,128)(2,1)}), bf16[16,256,256]{2,1,0:T(8,128)(2,1)}) %all-gather.8.cloned.1.call-update) | async-done | bytes 2097168 | tf_op jit(solution)/shard_map/all_gather | solution.py:37
  206.6 3.2 %gather_fusion.2 = bf16[8,256,256]{2,1,0:T(8,128)(2,1)} fusion(bf16[16,256,256]{2,1,0:T(8,128)(2,1)} %all-gather.8.cloned.1.call-done, s32[1024]{0:T(1024)S(1)} %pad_clamp_fusion), kind=kCustom, calls=%fused_computation.2 | custom fusion | bytes 2097184 | tf_op jit(solution)/shard_map/gather | solution.py:38
  209.8 0.0 copy-start.3
  209.8 3.3 %fusion.8 = f32[4,256,256]{2,1,0:T(8,128)} fusion(bf16[2,4,256,256]{3,2,1,0:T(8,128)(2,1)} %bitcast.197, bf16[1,2,4,256,256]{4,3,2,1,0:T(8,128)(2,1)S(1)} %copy-done, bf16[1,2,4,256,256]{4,3,2,1,0:T(8,128)(2,1)} %param.13), kind=kOutput, calls=%fused_computation.27 | convolution fusion | flops 537395200 | bytes 4194304 | tf_op jit(solution)/shard_map/btik,btkl->til/dot_general | solution.py:43
  213.2 0.0 copy-done.3
  213.2 4.2 %multiply_reduce_fusion = (f32[]{:T(128)}, f32[]{:T(128)}, f32[]{:T(128)}, f32[4,256,256]{2,1,0:T(8,128)}) fusion(f32[4,256,256]{2,1,0:T(8,128)} %get-tuple-element.28, f32[4,256]{1,0:T(4,128)S(1)} %fusion.59, f32[4,256,256]{2,1,0:T(8,128)} %fusion.8, bf16[2,4,256,256]{2,3,0,1:T(8,128)(2,1)S(1)} %copy-done.3, bf16[1,2,4,256,256]{3,4,1,2,0:T(8,128)(2,1)S(1)} %copy.22, ...), kind=kOutput, calls=%fused_computation.49 | convolution fusion | flops 539754496 | bytes 5771276 | tf_op jit(solution)/shard_map/atik,atkl->til/dot_general | solution.py:36
  217.3 8.4 %all-reduce = (f32[]{:T(128)}, f32[]{:T(128)}, f32[]{:T(128)}) all-reduce(f32[]{:T(128)} %get-tuple-element.13, f32[]{:T(128)} %get-tuple-element.12, f32[]{:T(128)} %get-tuple-element.11), channel_id=1, replica_groups=mesh['chain'=8,'sector'=4] {'sector'}, use_global_device_ids=true, to_apply=%region_15.0 | all-reduce | flops 3 | bytes 24 | tf_op jit(solution)/shard_map/psum | solution.py:46
  230.9 2.3 subtract_divide_fusion
  233.3 0.0 copy-start.1
  233.3 1.8 fusion.9
  235.0 5.4 %collective-permute-start = (bf16[2,4,256,256]{2,3,0,1:T(8,128)(2,1)}, bf16[2,4,256,256]{2,3,0,1:T(8,128)(2,1)}, u32[]{:S(2)}, u32[]{:S(2)}) collective-permute-start(bf16[2,4,256,256]{2,3,0,1:T(8,128)(2,1)} %fusion.9), channel_id=1, source_target_pairs={{0,4},{4,8},{8,12},{12,16},{16,20},{20,24},{24,28},{1,5},{5,9},{9,... | collective-permute-start | bytes 3145736 | tf_op jit(solution)/shard_map/ppermute | solution.py:12
  240.5 2.3 copy.23
  242.8 0.0 copy-done.1
  242.8 2.9 %fusion.10 = bf16[2,4,256,256]{2,3,0,1:T(8,128)(2,1)} fusion(bf16[1,2,4,256,256]{3,4,1,2,0:T(8,128)(2,1)} %copy.23, f32[4,256,256]{2,1,0:T(8,128)S(1)} %subtract_divide_fusion), kind=kOutput, calls=%fused_computation.29 | convolution fusion | flops 538968064 | bytes 3145728 | tf_op jit(solution)/shard_map/tij,atjk->atik/dot_general | solution.py:65
  245.7 1.9 collective-permute-start.1
  247.6 4.9 %collective-permute-done = bf16[2,4,256,256]{2,3,0,1:T(8,128)(2,1)} collective-permute-done((bf16[2,4,256,256]{2,3,0,1:T(8,128)(2,1)}, bf16[2,4,256,256]{2,3,0,1:T(8,128)(2,1)}, u32[]{:S(2)}, u32[]{:S(2)}) %collective-permute-start) | collective-permute-done | bytes 1048608 | tf_op jit(solution)/shard_map/ppermute | solution.py:12
  252.5 2.8 %add_bitcast_fusion.1 = f32[1,2,4,256,256]{3,4,1,2,0:T(8,128)} fusion(bf16[2,4,256,256]{2,3,0,1:T(8,128)(2,1)} %collective-permute-done, bf16[1,2,4,256,256]{3,4,1,2,0:T(8,128)(2,1)S(1)} %copy.22), kind=kLoop, calls=%fused_computation.9 | loop fusion | flops 1572864 | bytes 4194304 | tf_op jit(solution)/shard_map/broadcast_in_dim | solution.py:72
  255.3 0.0 copy-start.4
  255.3 3.0 %copy.31 = f32[1,2,4,256,256]{4,3,2,1,0:T(8,128)} copy(f32[1,2,4,256,256]{3,4,1,2,0:T(8,128)} %add_bitcast_fusion.1) | data formatting | bytes 4194304
  258.3 7.0 %collective-permute-done.1 = bf16[2,4,256,256]{2,3,0,1:T(8,128)(2,1)S(1)} collective-permute-done((bf16[2,4,256,256]{2,3,0,1:T(8,128)(2,1)}, bf16[2,4,256,256]{2,3,0,1:T(8,128)(2,1)S(1)}, u32[]{:S(2)}, u32[]{:S(2)}) %collective-permute-start.1) | collective-permute-done | bytes 1048608 | tf_op jit(solution)/shard_map/ppermute | solution.py:12
  265.3 0.0 copy-done.4
  265.3 1.6 add_bitcast_fusion
  266.8 2.9 %copy.32 = f32[1,2,4,256,256]{4,3,2,1,0:T(8,128)} copy(f32[1,2,4,256,256]{3,4,1,2,0:T(8,128)} %add_bitcast_fusion) | data formatting | bytes 4194304
  (1 shorter events, 0.0 us)
Async XLA Ops:
  7.2 54.5 %copy-start = (bf16[1,2,4,256,256]{4,3,2,1,0:T(8,128)(2,1)S(1)}, bf16[1,2,4,256,256]{4,3,2,1,0:T(8,128)(2,1)}, u32[]{:S(2)}) copy-start(bf16[1,2,4,256,256]{4,3,2,1,0:T(8,128)(2,1)} %param.14) | copy-start | bytes 3145732
  7.2 3.2 %copy-start.7 = (s32[2,16]{1,0:T(2,128)S(1)}, s32[2,16]{1,0:T(2,128)}, u32[]{:S(2)}) copy-start(s32[2,16]{1,0:T(2,128)} %param.15) | copy-start | bytes 388
  7.2 3.4 %copy-start.6 = (f32[1,3]{1,0:T(1,128)S(1)}, f32[1,3]{1,0:T(1,128)}, u32[]{:S(2)}) copy-start(f32[1,3]{1,0:T(1,128)} %param.10) | copy-start | bytes 40
  7.2 5.7 %copy-start.5 = (bf16[1,2,4,256,256]{4,3,2,1,0:T(8,128)(2,1)S(1)}, bf16[1,2,4,256,256]{4,3,2,1,0:T(8,128)(2,1)}, u32[]{:S(2)}) copy-start(bf16[1,2,4,256,256]{4,3,2,1,0:T(8,128)(2,1)} %param.11) | copy-start | bytes 3145732
  7.2 51.3 %all-gather.4.cloned.1.call-start = ((), (), s32[]{:S(2)}) async-start(), calls=%async_computation | async-start | bytes 2621440 | tf_op jit(solution)/shard_map/all_gather | solution.py:37
  10.4 122.6 %all-gather.6.cloned.1.call-start = ((), (), s32[]{:S(2)}) async-start(), calls=%async_computation.1 | async-start | bytes 2621440 | tf_op jit(solution)/shard_map/all_gather | solution.py:37
  15.0 50.0 %copy-start.2 = (bf16[2,4,256,256]{2,3,0,1:T(8,128)(2,1)}, bf16[2,4,256,256]{2,3,0,1:T(8,128)(2,1)S(1)}, u32[]{:S(2)}) copy-start(bf16[2,4,256,256]{2,3,0,1:T(8,128)(2,1)S(1)} %copy.34) | copy-start | bytes 3145732
  86.6 120.1 %all-gather.8.cloned.1.call-start = ((), (), s32[]{:S(2)}) async-start(), calls=%async_computation.2 | async-start | bytes 2621440 | tf_op jit(solution)/shard_map/all_gather | solution.py:37
  209.8 3.3 %copy-start.3 = (bf16[2,4,256,256]{2,3,0,1:T(8,128)(2,1)S(1)}, bf16[2,4,256,256]{2,3,0,1:T(8,128)(2,1)}, u32[]{:S(2)}) copy-start(bf16[2,4,256,256]{2,3,0,1:T(8,128)(2,1)} %copy-done.2) | copy-start | bytes 3145732
  233.3 9.5 %copy-start.1 = (f32[4,256,256]{2,1,0:T(8,128)}, f32[4,256,256]{2,1,0:T(8,128)S(1)}, u32[]{:S(2)}) copy-start(f32[4,256,256]{2,1,0:T(8,128)S(1)} %subtract_divide_fusion) | copy-start | bytes 3145732
  235.0 17.5 %collective-permute-start = (bf16[2,4,256,256]{2,3,0,1:T(8,128)(2,1)}, bf16[2,4,256,256]{2,3,0,1:T(8,128)(2,1)}, u32[]{:S(2)}, u32[]{:S(2)}) collective-permute-start(bf16[2,4,256,256]{2,3,0,1:T(8,128)(2,1)} %fusion.9), channel_id=1, source_target_pairs={{0,4},{4,8},{8,12},{12,16},{16,20},{20,24},{24,28},{1,5},{5,9},{9,... | collective-permute-start | bytes 3145736 | tf_op jit(solution)/shard_map/ppermute | solution.py:12
  245.7 19.6 %collective-permute-start.1 = (bf16[2,4,256,256]{2,3,0,1:T(8,128)(2,1)}, bf16[2,4,256,256]{2,3,0,1:T(8,128)(2,1)S(1)}, u32[]{:S(2)}, u32[]{:S(2)}) collective-permute-start(bf16[2,4,256,256]{2,3,0,1:T(8,128)(2,1)} %fusion.10), channel_id=1, source_target_pairs={{4,0},{8,4},{12,8},{16,12},{20,16},{24,20},{28,24},{5,1},{9,5},{13... | collective-permute-start | bytes 3145736 | tf_op jit(solution)/shard_map/ppermute | solution.py:12
  255.3 10.0 %copy-start.4 = (bf16[1,2,4,256,256]{3,4,1,2,0:T(8,128)(2,1)S(1)}, bf16[1,2,4,256,256]{3,4,1,2,0:T(8,128)(2,1)}, u32[]{:S(2)}) copy-start(bf16[1,2,4,256,256]{3,4,1,2,0:T(8,128)(2,1)} %copy.23) | copy-start | bytes 3145732
Sparse Core Ops, SparseCore 0:
  10.5 48.0 all-gather.3
  86.7 46.1 all-gather.5
  160.4 46.1 all-gather.7
where the time goes:
time: 277 us; the launch traced here: 276 us
  waiting for transfers between devices  144 us (52%)
  between operations  34.9 us (13%)
  matrix products  27.7 us (10%)
  blocking collectives  25.1 us (9%)
  local copies, waits for them, and re-layouts  20.5 us (7%)
  other arithmetic  16.3 us (6%)
  starting transfers between devices  7.47 us (3%)
    all_gather x3, waiting for transfers between devices, on_device(): gathered = lax.all_gather(state_b, 'sector', axis=0, tiled=True)  132 us
    psum x3, blocking collectives, on_device(): lax.psum((jnp.sum(state * state), jnp.sum(state * image), jnp.sum(image *...  25.1 us
    dot_general x3, matrix products, on_device(): jnp.einsum('atik,atkl->til', inner, right_one, preferred_element_type=f32)  13.2 us
    ppermute x2, waiting for transfers between devices, from_behind(): lax.ppermute(value, axis, [(source, source + steps) for source in range(i...  11.9 us
    dot_general x3, matrix products, on_device(): jnp.einsum('btik,btkl->til', hop_inner, hop_second, preferred_element_typ...  9.81 us
    gather x3, local copies, waits for them, and re-layouts, on_device(): picked = gathered[sources]  9.51 us
    unnamed x20, local copies, waits for them, and re-layouts  8.71 us
    convert_element_type x3, other arithmetic, on_device(): state_b = state.astype(bf16)  8.68 us
  transfers between devices with their start and end apart: 5, of which 5 were waited for; matrix products, arithmetic and copies ran while one was open for 5% of the time, Pallas kernels for 0%

commit v1 on v0

v1 whole, which is shorter than its diff:
```python
import functools

import jax
import jax.numpy as jnp
from jax import lax
from jax.experimental import pallas as pl
from jax.experimental.pallas import tpu as pltpu
from jax.sharding import PartitionSpec as P

STEPS = 3
LANES = 128
F32 = jnp.float32
BF16 = jnp.bfloat16


def from_behind(value, axis, steps):
    count = lax.axis_size(axis)
    initial, last = (max(0, -steps), min(count, count - steps))
    return lax.ppermute(value, axis, [(source, source + steps) for source in range(initial, last)])


def dot(a, b):
    return jnp.dot(a, b, preferred_element_type=F32)


def mask_of(rank, size):
    rows = lax.broadcasted_iota(jnp.int32, (size, size), 0)
    cols = lax.broadcasted_iota(jnp.int32, (size, size), 1)
    return (rows < rank) & (cols < rank)


def weights(sums_ref, step_now):
    total = jnp.sum(sums_ref[...], axis=1, keepdims=True)
    self_dot, cross, image_dot = total[0:1], total[1:2], total[2:3]
    quotient = cross / self_dot
    state_resid = cross - quotient * self_dot
    resid_dot = image_dot - 2.0 * quotient * cross + quotient * quotient * self_dot
    new_dot = self_dot - 2.0 * step_now * state_resid + step_now * step_now * resid_dot
    norm = jnp.sqrt(new_dot)
    return (1.0 + step_now * quotient) / norm, -step_now / norm


def lane_sums(value):
    rows = jnp.sum(value, axis=0, keepdims=True)
    total = rows[:, 0:LANES]
    for at in range(LANES, rows.shape[1], LANES):
        total = total + rows[:, at : at + LANES]
    return total


def two_sided(left_ref, right_ref, blocks):
    total = None
    for term, block in enumerate(blocks):
        half = dot(left_ref[term, 0], block).astype(BF16)
        now = dot(half, right_ref[term, 0])
        total = now if total is None else total + now
    return total


def start_kernel(rank_ref, psi_ref, state_ref, block_ref):
    size = psi_ref.shape[-1]
    state = jnp.where(mask_of(rank_ref[pl.program_id(0)], size), psi_ref[0], 0.0)
    state_ref[0] = state
    block_ref[0] = state.astype(BF16)


def site_first_kernel(rank_ref, block_ref, left_ref, right_ref, out_ref):
    terms = left_ref.shape[0]
    out_ref[0] = two_sided(left_ref, right_ref, [block_ref[0]] * terms)


def site_kernel(step, rank_ref, step_ref, sums_ref, state_ref, image_ref, block_ref, left_ref, right_ref, state_out, out_ref):
    size = block_ref.shape[-1]
    terms = left_ref.shape[0]
    keep, turn = weights(sums_ref, step_ref[0, step])
    mask = mask_of(rank_ref[pl.program_id(0)], size)
    site = two_sided(left_ref, right_ref, [block_ref[0]] * terms)
    image = image_ref[0]
    state_out[0] = keep * state_ref[0] + turn * image
    out_ref[0] = keep * image + turn * jnp.where(mask, site, 0.0)


def hop_kernel(step, hops, rank_ref, source_ref, step_ref, *refs):
    picked = refs[:hops]
    left_ref, right_ref, state_ref, base_ref = refs[hops : hops + 4]
    refs = refs[hops + 4 :]
    at = pl.program_id(0)
    size = base_ref.shape[-1]
    mask = mask_of(rank_ref[at], size)
    hop = two_sided(left_ref, right_ref, [ref[0] for ref in picked])
    if step == 0:
        image_ref, block_ref, sums_out = refs
        image = jnp.where(mask, base_ref[0] + hop, 0.0)
    else:
        sums_ref, image_ref, block_ref, sums_out = refs
        _, turn = weights(sums_ref, step_ref[0, step - 1])
        image = base_ref[0] + turn * jnp.where(mask, hop, 0.0)
    image_ref[0] = image
    block_ref[0] = image.astype(BF16)
    state = state_ref[0]

    @pl.when(at == 0)
    def _():
        sums_out[...] = jnp.zeros_like(sums_out)

    sums_out[0:1] += lane_sums(state * state)
    sums_out[1:2] += lane_sums(state * image)
    sums_out[2:3] += lane_sums(image * image)


def last_kernel(step, step_ref, sums_ref, state_ref, image_ref, state_out, block_ref):
    keep, turn = weights(sums_ref, step_ref[0, step])
    state = keep * state_ref[0] + turn * image_ref[0]
    state_out[0] = state
    block_ref[0] = state.astype(BF16)


def merge_kernel(scale, from_left, from_right, left_next, right_next, left_own, right_own, left_out, right_out):
    contract_rows = (((0,), (0,)), ((), ()))
    contract_cols = (((1,), (1,)), ((), ()))
    a = from_left[0]
    b = from_right[0]
    for term in range(left_next.shape[0]):
        half = lax.dot_general(a, left_next[term, 0], contract_rows, preferred_element_type=F32).astype(BF16)
        left_out[term, 0] = left_own[term, 0].astype(F32) + scale * dot(half, a)
        half = lax.dot_general(right_next[term, 0], b, contract_cols, preferred_element_type=F32).astype(BF16)
        right_out[term, 0] = right_own[term, 0].astype(F32) + scale * dot(b, half)


def on_device(psi, kept_rank, step_size, left_env, right_env, hop_left, hop_right, hop_source):
    count, size = psi.shape[1], psi.shape[2]
    terms, hops = left_env.shape[1], hop_left.shape[1]
    chi_total = count * lax.axis_size("sector") * size
    first_sector = lax.axis_index("sector") * count
    sources = lax.dynamic_slice_in_dim(hop_source, first_sector, count, 1)
    rank = kept_rank[0]
    left_one, right_one = left_env[0], right_env[0]
    hop_first, hop_second = hop_left[0], hop_right[0]

    square = pl.BlockSpec((1, size, size), lambda t, *_: (t, 0, 0))
    pair = pl.BlockSpec((terms, 1, size, size), lambda t, *_: (0, t, 0, 0))
    hop_pair = pl.BlockSpec((hops, 1, size, size), lambda t, *_: (0, t, 0, 0))
    sums_spec = pl.BlockSpec((8, LANES), lambda t, *_: (0, 0))
    scalars = pl.BlockSpec(memory_space=pltpu.SMEM)
    block_f32 = jax.ShapeDtypeStruct((count, size, size), F32)
    block_b16 = jax.ShapeDtypeStruct((count, size, size), BF16)
    sums_shape = jax.ShapeDtypeStruct((8, LANES), F32)
    flop = 2 * size**3

    def call(body, prefetch, in_specs, out_specs, out_shape, flops, args):
        moved = sum(a.size * a.dtype.itemsize for a in args[prefetch:])
        moved += sum(s.size * s.dtype.itemsize for s in out_shape)
        return pl.pallas_call(
            body,
            grid_spec=pltpu.PrefetchScalarGridSpec(
                num_scalar_prefetch=prefetch, grid=(count,), in_specs=in_specs, out_specs=out_specs
            ),
            out_shape=out_shape,
            compiler_params=pltpu.CompilerParams(
                dimension_semantics=("arbitrary",), vmem_limit_bytes=32 * 1024 * 1024
            ),
            cost_estimate=pl.CostEstimate(flops=flops, bytes_accessed=moved, transcendentals=0),
        )(*args)

    state, block = call(
        start_kernel, 1, [square], [square, square], [block_f32, block_b16], 0, (rank, psi[0])
    )
    left_next = right_next = None
    sums = image = base = None
    for step in range(STEPS):
        gathered = lax.all_gather(block, "sector", axis=0, tiled=True)
        if step == 0:
            left_next = from_behind(left_one, "chain", 1)
            right_next = from_behind(right_one, "chain", -1)
            (base,) = call(
                site_first_kernel, 1, [square, pair, pair], [square], [block_f32],
                count * terms * 2 * flop, (rank, block, left_one, right_one),
            )
        else:
            state, base = call(
                functools.partial(site_kernel, step - 1), 2,
                [sums_spec, square, square, square, pair, pair], [square, square], [block_f32, block_f32],
                count * terms * 2 * flop,
                (rank, step_size, sums, state, image, block, left_one, right_one),
            )
        picked = [
            pl.BlockSpec((1, size, size), functools.partial(lambda hop, t, rank, src, *_: (src[hop, t], 0, 0), hop))
            for hop in range(hops)
        ]
        extra = [] if step == 0 else [sums]
        image, block, sums = call(
            functools.partial(hop_kernel, step, hops), 3,
            picked + [hop_pair, hop_pair, square, square] + [sums_spec] * len(extra),
            [square, square, sums_spec], [block_f32, block_b16, sums_shape],
            count * hops * 2 * flop,
            (rank, sources, step_size, *([gathered] * hops), hop_first, hop_second, state, base, *extra),
        )
        sums = lax.psum(sums, "sector")
    state, block = call(
        functools.partial(last_kernel, STEPS - 1), 1, [sums_spec, square, square], [square, square],
        [block_f32, block_b16], 0, (step_size, sums, state, image),
    )
    from_left = from_behind(block, "chain", 1)
    from_right = from_behind(block, "chain", -1)
    env_f32 = jax.ShapeDtypeStruct((terms, count, size, size), F32)
    merged_left, merged_right = call(
        functools.partial(merge_kernel, float(chi_total)), 0, [square, square, pair, pair, pair, pair],
        [pair, pair], [env_f32, env_f32], count * terms * 4 * flop,
        (from_left, from_right, left_next, right_next, left_one, right_one),
    )
    return (state[None], merged_left[None], merged_right[None])


def solution(mesh):
    placed = (
        P("chain", "sector", None, None),
        P("chain", "sector"),
        P("chain", None),
        P("chain", None, "sector", None, None),
        P("chain", None, "sector", None, None),
        P("chain", None, "sector", None, None),
        P("chain", None, "sector", None, None),
        P(),
    )
    return jax.shard_map(
        on_device,
        mesh=mesh,
        in_specs=placed,
        out_specs=(
            P("chain", "sector", None, None),
            P("chain", None, "sector", None, None),
            P("chain", None, "sector", None, None),
        ),
        check_vma=False,
    )
```

time: 277 us -> 223 us (0.81); the launches traced: 276 us -> 219 us
  waiting for transfers between devices: 144 us -> 102 us
  matrix products: 27.7 us -> 0 us
  Pallas kernels: 0 us -> 26.3 us
  between operations: 34.9 us -> 14 us
  local copies, waits for them, and re-layouts: 20.5 us -> 41.3 us
  other arithmetic: 16.3 us -> 0 us
  starting transfers between devices: 7.47 us -> 13.2 us
    all_gather x3, waiting for transfers between devices: 132 us -> 94.2 us  [on_device(): gathered = lax.all_gather(block, 'sector', axis=0, tiled=True)]
    unnamed x20 -> x86, local copies, waits for them, and re-layouts: 8.71 us -> 41.2 us
    dot_general x8 -> x0, matrix products: 27.7 us -> none  [the longest x3 13.2 us: on_device(): jnp.einsum('atik,atkl->til', inner, right_one, preferred_element_type=f32)]
    pallas_call x0 -> x9, Pallas kernels: none -> 26.3 us  [call(): pl.pallas_call(body, grid_spec=pltpu.PrefetchScalarGridSpec(num_scalar_pr...]
    convert_element_type x4 -> x0, other arithmetic: 9.54 us -> none  [the longest x3 8.68 us: on_device(): state_b = state.astype(bf16)]
    gather x3 -> x0, local copies, waits for them, and re-layouts: 9.51 us -> none  [on_device(): picked = gathered[sources]]
    ppermute x2 -> x4, starting transfers between devices: 7.35 us -> 13 us  [from_behind(): lax.ppermute(value, axis, [(source, source + steps) for source in range(i...]
    broadcast_in_dim x2 -> x0, other arithmetic: 4.36 us -> none  [on_device(): return (state[None], merged_left[None], merged_right[None])]
  transfers between devices with their start and end apart: 5 -> 7, of which waited for: 5 -> 4; matrix products, arithmetic and copies ran while one was open for 5% -> 0% of each run, Pallas kernels for 0% -> 6%
where the time goes in v1:
time: 223 us; the launch traced here: 219 us
  waiting for transfers between devices  102 us (46%)
  local copies, waits for them, and re-layouts  41.3 us (19%)
  Pallas kernels  26.3 us (12%)
  blocking collectives  22.7 us (10%)
  between operations  14 us (6%)
  starting transfers between devices  13.2 us (6%)
    all_gather x3, waiting for transfers between devices, on_device(): gathered = lax.all_gather(block, 'sector', axis=0, tiled=True)  94.2 us
    unnamed x86, local copies, waits for them, and re-layouts  41.2 us
    pallas_call x9, Pallas kernels, call(): pl.pallas_call(body, grid_spec=pltpu.PrefetchScalarGridSpec(num_scalar_pr...  26.3 us
    psum x3, blocking collectives, on_device(): sums = lax.psum(sums, 'sector')  22.7 us
    ppermute x4, starting transfers between devices, from_behind(): lax.ppermute(value, axis, [(source, source + steps) for source in range(i...  13 us
    ppermute x4, waiting for transfers between devices, from_behind(): lax.ppermute(value, axis, [(source, source + steps) for source in range(i...  7.67 us
  transfers between devices with their start and end apart: 7, of which 4 were waited for; matrix products, arithmetic and copies ran while one was open for 0% of the time, Pallas kernels for 6%

profile of v1, /device:TPU:1, one launch (start us, length us, event | category | flops | bytes accessed | tf_op | source)
XLA Modules:
  0.0 219.4 jit_solution(16733389665652129536)
XLA Ops:
  7.2 0.0 all-gather.4.cloned.1.call-start
  7.2 1.3 copy-done.34
  8.5 0.7 copy-done.39
  9.2 0.7 shard_map.103
  10.0 1.0 copy-done.14
  10.9 0.8 copy-done.26
  11.7 0.0 all-gather.4.cloned.1.call-update
  11.7 0.0 all-gather.6.cloned.1.call-start
  11.8 1.2 copy-done.2
  13.0 1.0 copy-done.27
  14.1 0.7 copy-done.40
  14.7 2.6 %shard_map.104.refs_5_ = f32[4,256,256]{2,1,0:T(8,128)S(1)} custom-call(s32[4]{0:T(128)S(1)} %bitcast.27, bf16[4,256,256]{2,1,0:T(8,128)(2,1)S(1)} %copy-done.27, bf16[2,4,256,256]{3,2,1,0:T(8,128)(2,1)S(1)} %bitcast.9, bf16[2,4,256,256]{3,2,1,0:T(8,128)(2,1)S(1)} %bitcast.14), custom_call_target="tpu_custom_call" | custom-call | flops 536870912 | bytes 3670016 | tf_op jit(solution)/shard_map/pallas_call | solution.py:153
  17.4 1.0 copy-done.20
  18.4 0.1 constant_dynamic-slice_fusion.source_ref
  18.4 41.5 %all-gather.4.cloned.1.call-done.refs_0_.refs_1_ = bf16[16,256,256]{2,1,0:T(8,128)(2,1)} async-done(((bf16[4,256,256]{2,1,0:T(8,128)(2,1)}), bf16[16,256,256]{2,1,0:T(8,128)(2,1)}) %all-gather.4.cloned.1.call-update) | async-done | bytes 2097168 | tf_op jit(solution)/shard_map/all_gather | solution.py:171
  59.9 1.2 copy-done.5
  61.2 1.6 copy-done.8
  62.8 1.2 copy-done.15
  64.0 1.2 copy-done.21
  65.2 3.0 %shard_map.105 = (f32[4,256,256]{2,1,0:T(8,128)S(1)}, bf16[4,256,256]{2,1,0:T(8,128)(2,1)S(1)}, f32[8,128]{1,0:T(8,128)S(1)}) custom-call(s32[4]{0:T(128)S(1)} %bitcast.28, s32[2,4]{1,0:T(2,128)S(1)} %constant_dynamic-slice_fusion.source_ref, f32[1,3]{1,0:T(1,128)S(1)} %copy-done.42, bf16[16,256,256]{2,1,0:T(8,128)(2,1)S(1)} %copy-done.8, ...), custom_call_target="tpu_custom_call" | custom-call | flops 536870912 | bytes 9965568 | tf_op jit(solution)/shard_map/pallas_call | solution.py:153
  68.2 0.8 copy-done.24
  69.0 1.0 copy-done.37
  70.0 0.0 all-gather.6.cloned.1.call-update
  70.0 0.0 all-gather.8.cloned.1.call-start
  70.0 7.7 %psum.21.sums_ref.refs_6_ = f32[8,128]{1,0:T(8,128)S(1)} all-reduce(f32[8,128]{1,0:T(8,128)S(1)} %get-tuple-element.24), channel_id=1, replica_groups=mesh['chain'=8,'sector'=4] {'sector'}, use_global_device_ids=true, to_apply=%region_0.0 | all-reduce | flops 1024 | bytes 8192 | tf_op jit(solution)/shard_map/psum | solution.py:198
  77.8 1.3 copy-done.16
  79.0 1.0 copy-done.25
  80.1 1.2 copy-done.38
  81.3 2.7 %shard_map.106 = (f32[4,256,256]{2,1,0:T(8,128)S(1)}, f32[4,256,256]{2,1,0:T(8,128)S(1)}) custom-call(s32[4]{0:T(128)S(1)} %bitcast.29, f32[1,3]{1,0:T(1,128)S(1)} %copy-done.42, f32[8,128]{1,0:T(8,128)S(1)} %psum.21.sums_ref.refs_6_, f32[4,256,256]{2,1,0:T(8,128)S(1)} %copy-done.16, f32[4,256,256]{2,1,0:T(8,128)S(1)} %copy-done.38, ...), custom_call_target="tpu_custom_call" | custom-call | flops 536870912 | bytes 6819840 | tf_op jit(solution)/shard_map/pallas_call | solution.py:153
  84.0 1.0 copy-done.17
  85.0 1.0 copy-done.30
  85.9 28.9 %all-gather.6.cloned.1.call-done.refs_0_.refs_1_ = bf16[16,256,256]{2,1,0:T(8,128)(2,1)} async-done(((bf16[4,256,256]{2,1,0:T(8,128)(2,1)}), bf16[16,256,256]{2,1,0:T(8,128)(2,1)}) %all-gather.6.cloned.1.call-update) | async-done | bytes 2097168 | tf_op jit(solution)/shard_map/all_gather | solution.py:171
  114.8 1.2 copy-done.6
  116.0 1.6 copy-done.10
  117.6 1.2 copy-done.18
  118.8 1.2 copy-done.31
  120.1 3.0 %shard_map.107 = (f32[4,256,256]{2,1,0:T(8,128)S(1)}, bf16[4,256,256]{2,1,0:T(8,128)(2,1)S(1)}, f32[8,128]{1,0:T(8,128)S(1)}) custom-call(s32[4]{0:T(128)S(1)} %bitcast.30, s32[2,4]{1,0:T(2,128)S(1)} %constant_dynamic-slice_fusion.source_ref, f32[1,3]{1,0:T(1,128)S(1)} %copy-done.42, bf16[16,256,256]{2,1,0:T(8,128)(2,1)S(1)} %copy-done.10, ...), custom_call_target="tpu_custom_call" | custom-call | flops 536870912 | bytes 9969664 | tf_op jit(solution)/shard_map/pallas_call | solution.py:153
  123.1 0.8 copy-done.22
  123.9 1.0 copy-done.35
  124.8 0.0 all-gather.8.cloned.1.call-update
  124.8 3.7 %collective-permute-start.2 = (bf16[2,4,256,256]{3,2,1,0:T(8,128)(2,1)S(1)}, bf16[2,4,256,256]{3,2,1,0:T(8,128)(2,1)}, u32[]{:S(2)}, u32[]{:S(2)}) collective-permute-start(bf16[2,4,256,256]{3,2,1,0:T(8,128)(2,1)S(1)} %bitcast.11), channel_id=1, source_target_pairs={{0,4},{4,8},{8,12},{12,16},{16,20},{20,24},{24,28},{1,5},{5,9},{9,... | collective-permute-start | bytes 3145736 | tf_op jit(solution)/shard_map/ppermute | solution.py:19
  128.5 1.9 collective-permute-start.3
  130.5 7.6 %psum.22.sums_ref.refs_6_ = f32[8,128]{1,0:T(8,128)S(1)} all-reduce(f32[8,128]{1,0:T(8,128)S(1)} %get-tuple-element.29), channel_id=1, replica_groups=mesh['chain'=8,'sector'=4] {'sector'}, use_global_device_ids=true, to_apply=%region_1.0 | all-reduce | flops 1024 | bytes 8192 | tf_op jit(solution)/shard_map/psum | solution.py:198
  138.1 1.2 copy-done.19
  139.3 1.0 copy-done.23
  140.4 1.2 copy-done.36
  141.6 2.7 %shard_map.108 = (f32[4,256,256]{2,1,0:T(8,128)S(1)}, f32[4,256,256]{2,1,0:T(8,128)S(1)}) custom-call(s32[4]{0:T(128)S(1)} %bitcast.31, f32[1,3]{1,0:T(1,128)S(1)} %copy-done.42, f32[8,128]{1,0:T(8,128)S(1)} %psum.22.sums_ref.refs_6_, f32[4,256,256]{2,1,0:T(8,128)S(1)} %copy-done.19, f32[4,256,256]{2,1,0:T(8,128)S(1)} %copy-done.36, ...), custom_call_target="tpu_custom_call" | custom-call | flops 536870912 | bytes 6819840 | tf_op jit(solution)/shard_map/pallas_call | solution.py:153
  144.3 1.0 copy-done.11
  145.3 1.0 copy-done.28
  146.3 23.8 %all-gather.8.cloned.1.call-done.refs_0_.refs_1_ = bf16[16,256,256]{2,1,0:T(8,128)(2,1)} async-done(((bf16[4,256,256]{2,1,0:T(8,128)(2,1)}), bf16[16,256,256]{2,1,0:T(8,128)(2,1)}) %all-gather.8.cloned.1.call-update) | async-done | bytes 2097168 | tf_op jit(solution)/shard_map/all_gather | solution.py:171
  170.1 1.2 copy-done.7
  171.3 1.6 copy-done.9
  172.9 1.2 copy-done.12
  174.1 1.2 copy-done.29
  175.3 3.6 %shard_map.109 = (f32[4,256,256]{2,1,0:T(8,128)S(1)}, bf16[4,256,256]{2,1,0:T(8,128)(2,1)}, f32[8,128]{1,0:T(8,128)S(1)}) custom-call(s32[4]{0:T(128)S(1)} %bitcast.32, s32[2,4]{1,0:T(2,128)S(1)} %constant_dynamic-slice_fusion.source_ref, f32[1,3]{1,0:T(1,128)S(1)} %copy-done.42, bf16[16,256,256]{2,1,0:T(8,128)(2,1)S(1)} %copy-done.9, ...), custom_call_target="tpu_custom_call" | custom-call | flops 536870912 | bytes 9969664 | tf_op jit(solution)/shard_map/pallas_call | solution.py:153
  178.9 1.0 copy-done.32
  179.9 7.4 %psum.23.sums_ref = f32[8,128]{1,0:T(8,128)S(1)} all-reduce(f32[8,128]{1,0:T(8,128)S(1)} %get-tuple-element.33), channel_id=1, replica_groups=mesh['chain'=8,'sector'=4] {'sector'}, use_global_device_ids=true, to_apply=%region_2.0 | all-reduce | flops 1024 | bytes 8192 | tf_op jit(solution)/shard_map/psum | solution.py:198
  187.3 1.2 copy-done.13
  188.5 1.2 copy-done.33
  189.7 2.6 %shard_map.110 = (f32[4,256,256]{2,1,0:T(8,128)}, bf16[4,256,256]{2,1,0:T(8,128)(2,1)S(1)}) custom-call(f32[1,3]{1,0:T(1,128)S(1)} %copy-done.42, f32[8,128]{1,0:T(8,128)S(1)} %psum.23.sums_ref, f32[4,256,256]{2,1,0:T(8,128)S(1)} %copy-done.13, f32[4,256,256]{2,1,0:T(8,128)S(1)} %copy-done.33), custom_call_target="tpu_custom_call" | custom-call | bytes 3674112 | tf_op jit(solution)/shard_map/pallas_call | solution.py:153
  192.3 4.4 %collective-permute-start.1 = (bf16[4,256,256]{2,1,0:T(8,128)(2,1)S(1)}, bf16[4,256,256]{2,1,0:T(8,128)(2,1)S(1)}, u32[]{:S(2)}, u32[]{:S(2)}) collective-permute-start(bf16[4,256,256]{2,1,0:T(8,128)(2,1)S(1)} %get-tuple-element.36), channel_id=1, source_target_pairs={{4,0},{8,4},{12,8},{16,12},{20,16},{24,20},{28,24},{5,1},{9,5},{13... | collective-permute-start | bytes 1572872 | tf_op jit(solution)/shard_map/ppermute | solution.py:19
  196.7 3.1 %collective-permute-start = (bf16[4,256,256]{2,1,0:T(8,128)(2,1)S(1)}, bf16[4,256,256]{2,1,0:T(8,128)(2,1)S(1)}, u32[]{:S(2)}, u32[]{:S(2)}) collective-permute-start(bf16[4,256,256]{2,1,0:T(8,128)(2,1)S(1)} %get-tuple-element.36), channel_id=1, source_target_pairs={{0,4},{4,8},{8,12},{12,16},{16,20},{20,24},{24,28},{1,5},{5,9},{9,... | collective-permute-start | bytes 1572872 | tf_op jit(solution)/shard_map/ppermute | solution.py:19
  199.8 7.7 %collective-permute-done.1.from_right = bf16[4,256,256]{2,1,0:T(8,128)(2,1)S(1)} collective-permute-done((bf16[4,256,256]{2,1,0:T(8,128)(2,1)S(1)}, bf16[4,256,256]{2,1,0:T(8,128)(2,1)S(1)}, u32[]{:S(2)}, u32[]{:S(2)}) %collective-permute-start.1) | collective-permute-done | bytes 524320 | tf_op jit(solution)/shard_map/ppermute | solution.py:19
  207.4 5.4 %shard_map.111 = (f32[2,4,256,256]{3,2,1,0:T(8,128)}, f32[2,4,256,256]{3,2,1,0:T(8,128)}) custom-call(bf16[4,256,256]{2,1,0:T(8,128)(2,1)S(1)} %collective-permute-done.from_left, bf16[4,256,256]{2,1,0:T(8,128)(2,1)S(1)} %collective-permute-done.1.from_right, bf16[2,4,256,256]{3,2,1,0:T(8,128)(2,1)} %collective-permute-done.2.left_next, ...), custom_call_target="tpu_custom_call" | custom-call | flops 1073741824 | bytes 9437184 | tf_op jit(solution)/shard_map/pallas_call | solution.py:153
  (52 shorter events, 0.1 us)
Async XLA Ops:
  7.2 11.2 %copy-start = (s32[2,16]{1,0:T(2,128)S(1)}, s32[2,16]{1,0:T(2,128)}, u32[]{:S(2)}) copy-start(s32[2,16]{1,0:T(2,128)} %param.15) | copy-start | bytes 388
  7.2 4.6 %copy-start.1 = (bf16[1,2,4,256,256]{4,3,2,1,0:T(8,128)(2,1)S(1)}, bf16[1,2,4,256,256]{4,3,2,1,0:T(8,128)(2,1)}, u32[]{:S(2)}) copy-start(bf16[1,2,4,256,256]{4,3,2,1,0:T(8,128)(2,1)} %param.11) | copy-start | bytes 3145732
  7.2 52.7 %all-gather.4.cloned.1.call-start = ((), (), s32[]{:S(2)}) async-start(), calls=%async_computation | async-start | bytes 2621440 | tf_op jit(solution)/shard_map/all_gather | solution.py:171
  7.2 1.3 copy-start.34
  8.5 0.7 copy-start.39
  10.0 1.0 copy-start.14
  10.9 0.8 copy-start.26
  11.7 48.2 %copy-start.41 = (s32[1,4]{1,0:T(1,128)S(1)}, s32[1,4]{1,0:T(1,128)}, u32[]{:S(2)}) copy-start(s32[1,4]{1,0:T(1,128)} %param.9) | copy-start | bytes 52
  11.7 48.2 %copy-start.42 = (f32[1,3]{1,0:T(1,128)S(1)}, f32[1,3]{1,0:T(1,128)}, u32[]{:S(2)}) copy-start(f32[1,3]{1,0:T(1,128)} %step_ref.11) | copy-start | bytes 40
  11.7 103.0 %all-gather.6.cloned.1.call-start = ((), (), s32[]{:S(2)}) async-start(), calls=%async_computation.1 | async-start | bytes 2621440 | tf_op jit(solution)/shard_map/all_gather | solution.py:171
  11.8 1.2 copy-start.2
  13.0 1.0 copy-start.27
  14.1 0.7 copy-start.40
  14.7 45.2 %copy-start.4 = (bf16[1,2,4,256,256]{4,3,2,1,0:T(8,128)(2,1)S(1)}, bf16[1,2,4,256,256]{4,3,2,1,0:T(8,128)(2,1)}, u32[]{:S(2)}) copy-start(bf16[1,2,4,256,256]{4,3,2,1,0:T(8,128)(2,1)} %param.13) | copy-start | bytes 3145732
  17.4 1.0 copy-start.20
  59.9 1.2 copy-start.5
  61.2 1.6 copy-start.8
  62.7 1.2 copy-start.15
  64.0 1.2 copy-start.21
  65.2 12.5 %copy-start.3 = (bf16[1,2,4,256,256]{4,3,2,1,0:T(8,128)(2,1)S(1)}, bf16[1,2,4,256,256]{4,3,2,1,0:T(8,128)(2,1)}, u32[]{:S(2)}) copy-start(bf16[1,2,4,256,256]{4,3,2,1,0:T(8,128)(2,1)} %param.12) | copy-start | bytes 3145732
  68.2 0.8 copy-start.24
  69.0 1.0 copy-start.37
  70.0 100.1 %all-gather.8.cloned.1.call-start = ((), (), s32[]{:S(2)}) async-start(), calls=%async_computation.2 | async-start | bytes 2621440 | tf_op jit(solution)/shard_map/all_gather | solution.py:171
  77.7 1.3 copy-start.16
  79.0 1.0 copy-start.25
  80.1 1.2 copy-start.38
  84.0 1.0 copy-start.17
  85.0 1.0 copy-start.30
  114.8 1.2 copy-start.6
  116.0 1.6 copy-start.10
  117.6 1.2 copy-start.18
  118.8 1.2 copy-start.31
  123.1 0.8 copy-start.22
  123.9 1.0 copy-start.35
  124.8 74.9 %collective-permute-start.2 = (bf16[2,4,256,256]{3,2,1,0:T(8,128)(2,1)S(1)}, bf16[2,4,256,256]{3,2,1,0:T(8,128)(2,1)}, u32[]{:S(2)}, u32[]{:S(2)}) collective-permute-start(bf16[2,4,256,256]{3,2,1,0:T(8,128)(2,1)S(1)} %bitcast.11), channel_id=1, source_target_pairs={{0,4},{4,8},{8,12},{12,16},{16,20},{20,24},{24,28},{1,5},{5,9},{9,... | collective-permute-start | bytes 3145736 | tf_op jit(solution)/shard_map/ppermute | solution.py:19
  128.5 71.2 %collective-permute-start.3 = (bf16[2,4,256,256]{3,2,1,0:T(8,128)(2,1)S(1)}, bf16[2,4,256,256]{3,2,1,0:T(8,128)(2,1)}, u32[]{:S(2)}, u32[]{:S(2)}) collective-permute-start(bf16[2,4,256,256]{3,2,1,0:T(8,128)(2,1)S(1)} %bitcast.16), channel_id=1, source_target_pairs={{4,0},{8,4},{12,8},{16,12},{20,16},{24,20},{28,24},{5,1},{9,5},{13... | collective-permute-start | bytes 3145736 | tf_op jit(solution)/shard_map/ppermute | solution.py:19
  138.1 1.2 copy-start.19
  139.3 1.0 copy-start.23
  140.4 1.2 copy-start.36
  144.3 1.0 copy-start.11
  145.3 1.0 copy-start.28
  170.1 1.2 copy-start.7
  171.3 1.6 copy-start.9
  172.9 1.2 copy-start.12
  174.1 1.2 copy-start.29
  178.9 1.0 copy-start.32
  187.3 1.2 copy-start.13
  188.5 1.2 copy-start.33
  192.3 15.1 %collective-permute-start.1 = (bf16[4,256,256]{2,1,0:T(8,128)(2,1)S(1)}, bf16[4,256,256]{2,1,0:T(8,128)(2,1)S(1)}, u32[]{:S(2)}, u32[]{:S(2)}) collective-permute-start(bf16[4,256,256]{2,1,0:T(8,128)(2,1)S(1)} %get-tuple-element.36), channel_id=1, source_target_pairs={{4,0},{8,4},{12,8},{16,12},{20,16},{24,20},{28,24},{5,1},{9,5},{13... | collective-permute-start | bytes 1572872 | tf_op jit(solution)/shard_map/ppermute | solution.py:19
  196.7 10.8 %collective-permute-start = (bf16[4,256,256]{2,1,0:T(8,128)(2,1)S(1)}, bf16[4,256,256]{2,1,0:T(8,128)(2,1)S(1)}, u32[]{:S(2)}, u32[]{:S(2)}) collective-permute-start(bf16[4,256,256]{2,1,0:T(8,128)(2,1)S(1)} %get-tuple-element.36), channel_id=1, source_target_pairs={{0,4},{4,8},{8,12},{12,16},{16,20},{20,24},{24,28},{1,5},{5,9},{9,... | collective-permute-start | bytes 1572872 | tf_op jit(solution)/shard_map/ppermute | solution.py:19
Sparse Core Ops, SparseCore 0:
  11.9 48.0 all-gather.3
  70.1 44.6 all-gather.5
  125.0 45.0 all-gather.7

commit v2 on v0

v2 whole, which is shorter than its diff:
```python
import functools

import jax
import jax.numpy as jnp
from jax import lax
from jax.experimental import pallas as pl
from jax.experimental.pallas import tpu as pltpu
from jax.sharding import PartitionSpec as P

STEPS = 3
LANES = 128
ROWS = 16
FAR = 1 << 20
F32 = jnp.float32
BF16 = jnp.bfloat16
I32 = jnp.int32
VMEM_BYTES = 56 * 1024 * 1024
PLANS = (
    (16, 11, 16),
    (17, 14, 17),
    (14, 18, 14),
    (22, 11, 22),
    (19, 16, 19),
    (19, 19, 19),
    (24, 17, 24),
    (17, 25, 17),
    (27, 22, 27),
    (32, 32, 32),
)


def from_behind(value, axis, steps):
    count = lax.axis_size(axis)
    initial, last = (max(0, -steps), min(count, count - steps))
    return lax.ppermute(value, axis, [(source, source + steps) for source in range(initial, last)])


def cyclic(value, axis, shift):
    count = lax.axis_size(axis)
    return lax.ppermute(value, axis, [(source, (source + shift) % count) for source in range(count)])


def dot(a, b):
    return jnp.dot(a, b, preferred_element_type=F32)


def mask_of(rank, size):
    rows = lax.broadcasted_iota(I32, (size, size), 0)
    cols = lax.broadcasted_iota(I32, (size, size), 1)
    return (rows < rank) & (cols < rank)


def weights(sums, step_now):
    total = jnp.sum(sums, axis=1, keepdims=True)
    self_dot, cross, image_dot = total[0:1], total[1:2], total[2:3]
    quotient = cross / self_dot
    state_resid = cross - quotient * self_dot
    resid_dot = image_dot - 2.0 * quotient * cross + quotient * quotient * self_dot
    new_dot = self_dot - 2.0 * step_now * state_resid + step_now * step_now * resid_dot
    norm = jnp.sqrt(new_dot)
    return (1.0 + step_now * quotient) / norm, -step_now / norm


def lane_sums(value):
    rows = jnp.sum(value, axis=0, keepdims=True)
    total = rows[:, 0:LANES]
    for at in range(LANES, rows.shape[1], LANES):
        total = total + rows[:, at : at + LANES]
    return total


def head_of(rows, room_ref):
    room_ref[...] = jnp.zeros_like(room_ref)
    for place, row in enumerate(rows):
        for part in range(3):
            now = row.astype(BF16).astype(F32)
            room_ref[3 * part + place : 3 * part + place + 1] = now
            row = row - now
    return room_ref[...].astype(BF16)


def rows_of_head(head, room_ref):
    room_ref[...] = head.astype(F32)
    return room_ref[0:3] + room_ref[3:6] + room_ref[6:9]


def kept_rows(rank):
    return (rank + (ROWS - 1)) & ~(ROWS - 1)


def packed_rows(rank, half):
    rows = kept_rows(rank)
    return jnp.where(rows <= half, rows, 3 * rows - 2 * half)


def at_rows(ref, start, rows):
    return ref.at[pl.ds(pl.multiple_of(start, ROWS), rows), :]


def quarters(value):
    half = value.shape[0] // 2
    return (
        value[:half, :half].astype(BF16),
        value[:half, half:].T.astype(BF16),
        value[half:, :half].astype(BF16),
        value[half:, half:].astype(BF16),
    )


def put_packed(ref, start, rank, parts):
    half = parts[0].shape[0]
    over = jnp.maximum(kept_rows(rank) - half, 0)
    for place, part in zip((0, half, half + over, half + 2 * over), parts):
        at_rows(ref, start + place, half)[...] = part


def get_packed(ref, start, rank, half):
    kept = kept_rows(rank)
    over = jnp.maximum(kept - half, 0)
    row = lax.broadcasted_iota(I32, (half, half), 0)

    def part(place, rows):
        value = at_rows(ref, start + place, half)[...].astype(F32)
        return jnp.where(row < rows, value, 0.0)

    first = part(0, kept).astype(BF16)
    second = part(half, over).T.astype(BF16)
    third = part(half + over, over).astype(BF16)
    fourth = part(half + 2 * over, over).astype(BF16)
    top = jnp.concatenate([first, second], axis=1)
    low = jnp.concatenate([third, fourth], axis=1)
    return jnp.concatenate([top, low], axis=0)


class Layout:
    def __init__(self, ways, count, hops):
        self.ways, self.count, self.hops = ways, count, hops
        self.plan = 0
        self.rank = 1
        self.send = self.rank + count
        self.shift = self.send + (ways - 1) * count
        self.start = self.shift + hops * count
        self.source_rank = self.start + hops * count
        self.size = self.source_rank + hops * count


def plan_kernel(lay, half, plans, me_ref, source_ref, *refs):
    ways, count, hops = lay.ways, lay.count, lay.hops
    rank_refs, (table_ref, need_ref, place_ref, all_ref) = refs[:ways], refs[ways:]
    me = me_ref[0]
    for at in range(ways * count * ways):
        need_ref[at] = 0
    for shift in range(ways):
        owner = lax.rem(me + (ways - shift), ways)
        for at in range(count):
            all_ref[owner * count + at] = rank_refs[shift][at]
    for hop in range(hops):
        for taker in range(ways):
            for at in range(count):
                need_ref[source_ref[hop, taker * count + at] * ways + taker] = 1
    largest = [jnp.int32(0)] * ways
    for owner in range(ways):
        for taker in range(ways):
            if owner == taker:
                continue
            shift = (taker - owner) % ways
            used = jnp.int32(ROWS)
            for at in range(count):
                source = owner * count + at
                needed = need_ref[source * ways + taker] == 1
                rows = packed_rows(all_ref[source], half)

                @pl.when(owner == me)
                def _():
                    table_ref[lay.send + (shift - 1) * count + at] = jnp.where(needed, used, FAR)

                @pl.when(taker == me)
                def _():
                    place_ref[source] = used

                used = used + jnp.where(needed, rows, 0)
            largest[shift] = jnp.maximum(largest[shift], used)
    chosen = jnp.int32(len(plans) - 1)
    for index in reversed(range(len(plans) - 1)):
        fits = largest[1] <= plans[index][0]
        for shift in range(2, ways):
            fits = fits & (largest[shift] <= plans[index][shift - 1])
        chosen = jnp.where(fits, index, chosen)
    table_ref[lay.plan] = chosen
    for at in range(count):
        table_ref[lay.rank + at] = rank_refs[0][at]
        for hop in range(hops):
            source = source_ref[hop, me * count + at]
            owner = lax.div(source, count)
            here = owner == me
            slot = hop * count + at
            table_ref[lay.shift + slot] = lax.rem(me + (ways - owner), ways)
            table_ref[lay.start + slot] = jnp.where(here, (source - owner * count) * (4 * half), place_ref[source])
            table_ref[lay.source_rank + slot] = all_ref[source]


def fill_sends(lay, half, caps, table_ref, at, own_buf, send_bufs):
    packed = at_rows(own_buf, at * 4 * half, 4 * half)[...]
    for shift in range(1, lay.ways):
        start = jnp.minimum(table_ref[lay.send + (shift - 1) * lay.count + at], caps[shift - 1])
        at_rows(send_bufs[shift - 1], start, 4 * half)[...] = packed


def send_copies(send_bufs, send_outs, sems):
    return [
        pltpu.make_async_copy(buf.at[pl.ds(0, out.shape[0]), :], out, sems.at[at])
        for at, (buf, out) in enumerate(zip(send_bufs, send_outs))
    ]


def prepare_kernel(half, rank_ref, psi_ref, state_ref, own_ref):
    rank = rank_ref[pl.program_id(0)]
    value = jnp.where(mask_of(rank, 2 * half), psi_ref[0], 0.0)
    state_ref[0] = value
    put_packed(own_ref, 0, rank, quarters(value))


def send_kernel(lay, half, caps, table_ref, own_ref, *refs):
    number = lay.ways - 1
    send_outs, send_bufs, sems = refs[:number], refs[number : 2 * number], refs[2 * number]
    for buf in send_bufs:
        buf[0:ROWS] = jnp.zeros((ROWS, half), BF16)

    @pl.loop(0, lay.count)
    def _(at):
        fill_sends(lay, half, caps, table_ref, at, own_ref, send_bufs)

    copies = send_copies(send_bufs, send_outs, sems)
    for copy in copies:
        copy.start()
    for copy in copies:
        copy.wait()


def two_sided(left_ref, right_ref, blocks):
    total = None
    for term, block in enumerate(blocks):
        part = dot(left_ref[term, 0], block).astype(BF16)
        now = dot(part, right_ref[term, 0])
        total = now if total is None else total + now
    return total


def site_kernel(lay, half, table_ref, own_ref, left_ref, right_ref, out_ref):
    block = get_packed(own_ref, 0, table_ref[lay.rank + pl.program_id(0)], half)
    out_ref[0] = two_sided(left_ref, right_ref, [block] * left_ref.shape[0])


def hop_kernel(lay, half, caps, table_ref, turn_ref, step_ref, sums_ref, *refs):
    ways, count, hops = lay.ways, lay.count, lay.hops
    size = 2 * half
    refs = list(refs)

    def take(number):
        out = refs[:number]
        del refs[:number]
        return out

    own_in, *packed_in = take(ways)
    left_in, right_in, site_in, state_in, image_in = take(5)
    state_out, image_out, sums_out = take(3)
    own_out, *send_outs = take(ways)
    pool, left, right, site, state, image, room, sems, out_sems = take(9)
    own_buf, *send_bufs = take(ways)

    places = [0, own_in.shape[0]]
    for cap in caps:
        places.append(places[-1] + cap)
    arrivals = [
        pltpu.make_async_copy(ref, pool.at[pl.ds(place, ref.shape[0]), :], sems.at[0, at])
        for at, (ref, place) in enumerate(zip([own_in, *packed_in], places))
    ]

    def inputs(at):
        return [
            pltpu.make_async_copy(left_in.at[:, at], left.at[:, at], sems.at[1, at]),
            pltpu.make_async_copy(right_in.at[:, at], right.at[:, at], sems.at[2, at]),
            pltpu.make_async_copy(site_in.at[at], site.at[at], sems.at[3, at]),
            pltpu.make_async_copy(state_in.at[at], state.at[at], sems.at[4, at]),
            pltpu.make_async_copy(image_in.at[at], image.at[at], sems.at[5, at]),
        ]

    def outputs(at):
        rows = pl.ds(pl.multiple_of(at * 4 * half, ROWS), 4 * half)
        return [
            pltpu.make_async_copy(state.at[at], state_out.at[at], out_sems.at[0, at]),
            pltpu.make_async_copy(image.at[at], image_out.at[at], out_sems.at[1, at]),
            pltpu.make_async_copy(own_buf.at[rows, :], own_out.at[rows, :], out_sems.at[2, at]),
        ]

    for copy in arrivals:
        copy.start()
    for at in range(count):
        for copy in inputs(at):
            copy.start()
    for copy in arrivals:
        copy.wait()

    sums = sums_ref[0:3]
    for place in places[1:ways]:
        sums = sums + rows_of_head(pool[place : place + ROWS], room)
    first = turn_ref[0] == 0
    keep, turn = weights(sums, step_ref[0, jnp.maximum(turn_ref[0] - 1, 0)])
    keep_state = jnp.where(first, 1.0, keep)
    keep_image = jnp.where(first, 0.0, keep)
    turn_state = jnp.where(first, 0.0, turn)
    turn_image = jnp.where(first, 1.0, turn)

    def sector(at, sums):
        for copy in inputs(at):
            copy.wait()
        total = site[at]
        for hop in range(hops):
            slot = hop * count + at
            shift = table_ref[lay.shift + slot]
            start = table_ref[lay.start + slot]
            for way in range(1, ways):
                start = start + jnp.where(shift == way, places[way], 0)
            block = get_packed(pool, start, table_ref[lay.source_rank + slot], half)
            part = dot(left[hop, at], block).astype(BF16)
            total = total + dot(part, right[hop, at])
        rank = table_ref[lay.rank + at]
        before = image[at]
        now = keep_state * state[at] + turn_state * before
        value = keep_image * before + turn_image * jnp.where(mask_of(rank, size), total, 0.0)
        state[at] = now
        image[at] = value
        put_packed(own_buf, at * 4 * half, rank, quarters(value))
        for copy in outputs(at):
            copy.start()
        fill_sends(lay, half, caps, table_ref, at, own_buf, send_bufs)
        return tuple(
            whole + lane_sums(part) for whole, part in zip(sums, (now * now, now * value, value * value))
        )

    rows = lax.fori_loop(0, count, sector, (jnp.zeros((1, LANES), F32),) * 3)
    head = head_of(rows, room)
    for buf in send_bufs:
        buf[0:ROWS] = head
    leaving = send_copies(send_bufs, send_outs, sems.at[0])
    for copy in leaving:
        copy.start()
    sums_out[...] = jnp.zeros_like(sums_out)
    for place, row in enumerate(rows):
        sums_out[place : place + 1] = row
    for copy in leaving:
        copy.wait()
    for at in range(count):
        for copy in outputs(at):
            copy.wait()


def last_kernel(step, step_ref, sums_ref, state_ref, image_ref, state_out, block_ref):
    keep, turn = weights(sums_ref[...], step_ref[0, step])
    state = keep * state_ref[0] + turn * image_ref[0]
    state_out[0] = state
    block_ref[0] = state.astype(BF16)


def merge_kernel(scale, from_left, from_right, left_next, right_next, left_own, right_own, left_out, right_out):
    contract_rows = (((0,), (0,)), ((), ()))
    contract_cols = (((1,), (1,)), ((), ()))
    a = from_left[0]
    b = from_right[0]
    for term in range(left_next.shape[0]):
        part = lax.dot_general(a, left_next[term, 0], contract_rows, preferred_element_type=F32).astype(BF16)
        left_out[term, 0] = left_own[term, 0].astype(F32) + scale * dot(part, a)
        part = lax.dot_general(right_next[term, 0], b, contract_cols, preferred_element_type=F32).astype(BF16)
        right_out[term, 0] = right_own[term, 0].astype(F32) + scale * dot(b, part)


def run_kernel(body, args, in_specs, out_shape, out_specs, *, flops=0, grid=(), scratch=(), reuse=None):
    moved = sum(a.size * a.dtype.itemsize for a in args)
    moved += sum(s.size * s.dtype.itemsize for s in out_shape)
    return pl.pallas_call(
        body,
        grid=grid,
        in_specs=in_specs,
        out_specs=out_specs,
        out_shape=out_shape,
        scratch_shapes=list(scratch),
        input_output_aliases=reuse or {},
        compiler_params=pltpu.CompilerParams(vmem_limit_bytes=VMEM_BYTES),
        cost_estimate=pl.CostEstimate(flops=flops, bytes_accessed=moved, transcendentals=0),
    )(*args)


def on_device(psi, kept_rank, step_size, left_env, right_env, hop_left, hop_right, hop_source):
    count, size = psi.shape[1], psi.shape[2]
    half = size // 2
    terms, hops = left_env.shape[1], hop_left.shape[1]
    ways = lax.axis_size("sector")
    chi_total = count * ways * size
    lay = Layout(ways, count, hops)
    left_one, right_one = left_env[0], right_env[0]
    hop_first, hop_second = hop_left[0], hop_right[0]
    full = count * 4 * half
    plans = [tuple(ROWS * (full * part // (32 * ROWS)) + (ROWS if part == 32 else 0) for part in plan) for plan in PLANS if len(plan) == ways - 1]
    if not plans:
        plans = [(full + ROWS,) * (ways - 1)]

    smem = pl.BlockSpec(memory_space=pltpu.SMEM)
    vmem = pl.BlockSpec(memory_space=pltpu.VMEM)
    anywhere = pl.BlockSpec(memory_space=pl.ANY)
    square = pl.BlockSpec((1, size, size), lambda t: (t, 0, 0))
    packed = pl.BlockSpec((4 * half, half), lambda t: (t, 0))
    pair = pl.BlockSpec((terms, 1, size, size), lambda t: (0, t, 0, 0))
    sums_spec = pl.BlockSpec((8, LANES), lambda t: (0, 0))
    block_f32 = jax.ShapeDtypeStruct((count, size, size), F32)
    block_b16 = jax.ShapeDtypeStruct((count, size, size), BF16)
    own_shape = jax.ShapeDtypeStruct((full, half), BF16)
    sums_shape = jax.ShapeDtypeStruct((8, LANES), F32)
    flop = 2 * size**3

    rank = kept_rank[0]
    ranks = [rank] + [cyclic(rank, "sector", shift) for shift in range(1, ways)]
    left_next = from_behind(left_one, "chain", 1)
    right_next = from_behind(right_one, "chain", -1)
    state, own = run_kernel(
        functools.partial(prepare_kernel, half),
        (rank, psi[0]),
        [smem, square],
        [block_f32, own_shape],
        [square, packed],
        grid=(count,),
    )
    me = lax.axis_index("sector").astype(I32).reshape(1)
    (table,) = run_kernel(
        functools.partial(plan_kernel, lay, half, plans),
        (me, hop_source, *ranks),
        [smem] * (2 + ways),
        [jax.ShapeDtypeStruct((lay.size,), I32)],
        [smem],
        scratch=[
            pltpu.SMEM((ways * count * ways,), I32),
            pltpu.SMEM((ways * count,), I32),
            pltpu.SMEM((ways * count,), I32),
        ],
    )

    def update(caps, state, own, table, step_size, left_one, right_one, hop_first, hop_second):
        send_shapes = [jax.ShapeDtypeStruct((cap, half), BF16) for cap in caps]
        bufs = [pltpu.VMEM((cap + 4 * half, half), BF16) for cap in caps]
        sends = run_kernel(
            functools.partial(send_kernel, lay, half, caps),
            (table, own),
            [smem, vmem],
            send_shapes,
            [anywhere] * (ways - 1),
            scratch=bufs + [pltpu.SemaphoreType.DMA((ways - 1,))],
        )

        def step(turn, carried):
            state, image, sums, own, *sends = carried
            arrived = [cyclic(send, "sector", 1 + at) for at, send in enumerate(sends)]
            (site,) = run_kernel(
                functools.partial(site_kernel, lay, half),
                (table, own, left_one, right_one),
                [smem, packed, pair, pair],
                [block_f32],
                [square],
                flops=count * terms * 2 * flop,
                grid=(count,),
            )
            outs = run_kernel(
                functools.partial(hop_kernel, lay, half, caps),
                (table, turn.reshape(1), step_size, sums, own, *arrived, hop_first, hop_second, site, state, image),
                [smem, smem, smem, vmem] + [anywhere] * (ways + 5),
                [block_f32, block_f32, sums_shape, own_shape, *send_shapes],
                [anywhere, anywhere, vmem] + [anywhere] * ways,
                flops=count * hops * 2 * flop,
                scratch=[
                    pltpu.VMEM((full + sum(caps) + 4 * half, half), BF16),
                    pltpu.VMEM((hops, count, size, size), BF16),
                    pltpu.VMEM((hops, count, size, size), BF16),
                    pltpu.VMEM((count, size, size), F32),
                    pltpu.VMEM((count, size, size), F32),
                    pltpu.VMEM((count, size, size), F32),
                    pltpu.VMEM((ROWS, half), F32),
                    pltpu.SemaphoreType.DMA((6, max(ways, count))),
                    pltpu.SemaphoreType.DMA((3, count)),
                    pltpu.VMEM((full, half), BF16),
                    *bufs,
                ],
                reuse={4: 3, 7 + ways: 0, 8 + ways: 1},
            )
            return list(outs)

        zeros = jnp.zeros((8, LANES), F32)
        state, image, sums, *_ = lax.fori_loop(0, step_size.shape[1], step, [state, state, zeros, own, *sends])
        return state, image, sums

    state, image, sums = lax.switch(
        table[lay.plan],
        [functools.partial(update, caps) for caps in plans],
        state, own, table, step_size, left_one, right_one, hop_first, hop_second,
    )
    sums = lax.psum(sums, "sector")
    state, block = run_kernel(
        functools.partial(last_kernel, STEPS - 1),
        (step_size, sums, state, image),
        [smem, sums_spec, square, square],
        [block_f32, block_b16],
        [square, square],
        grid=(count,),
    )
    from_left = from_behind(block, "chain", 1)
    from_right = from_behind(block, "chain", -1)
    env_f32 = jax.ShapeDtypeStruct((terms, count, size, size), F32)
    merged_left, merged_right = run_kernel(
        functools.partial(merge_kernel, float(chi_total)),
        (from_left, from_right, left_next, right_next, left_one, right_one),
        [square, square, pair, pair, pair, pair],
        [env_f32, env_f32],
        [pair, pair],
        flops=count * terms * 4 * flop,
        grid=(count,),
    )
    return (state[None], merged_left[None], merged_right[None])


def solution(mesh):
    placed = (
        P("chain", "sector", None, None),
        P("chain", "sector"),
        P("chain", None),
        P("chain", None, "sector", None, None),
        P("chain", None, "sector", None, None),
        P("chain", None, "sector", None, None),
        P("chain", None, "sector", None, None),
        P(),
    )
    return jax.shard_map(
        on_device,
        mesh=mesh,
        in_specs=placed,
        out_specs=(
            P("chain", "sector", None, None),
            P("chain", None, "sector", None, None),
            P("chain", None, "sector", None, None),
        ),
        check_vma=False,
    )
```

time: 277 us -> 164 us (0.59)
  waiting for transfers between devices: 144 us -> 36.6 us
  Pallas kernels: 0 us -> 51.6 us
  starting transfers between devices: 7.47 us -> 52.4 us
  between operations: 34.9 us -> 1.38 us
  matrix products: 27.7 us -> 0 us
  other arithmetic: 16.3 us -> 0 us
  blocking collectives: 25.1 us -> 9.76 us
  local copies, waits for them, and re-layouts: 20.5 us -> 9.36 us
    all_gather x3 -> x0, waiting for transfers between devices: 132 us -> none  [on_device(): gathered = lax.all_gather(state_b, 'sector', axis=0, tiled=True)]
    pallas_call x0 -> x11, Pallas kernels: none -> 51.6 us  [run_kernel(): pl.pallas_call(body, grid=grid, in_specs=in_specs, out_specs=out_specs, o...]
    dot_general x8 -> x0, matrix products: 27.7 us -> none  [the longest x3 13.2 us: on_device(): jnp.einsum('atik,atkl->til', inner, right_one, preferred_element_type=f32)]
    ppermute x2 -> x4, starting transfers between devices: 7.35 us -> 33.6 us  [from_behind(): lax.ppermute(value, axis, [(source, source + steps) for source in range(i...]
    ppermute x0 -> x12, waiting for transfers between devices: none -> 23.4 us  [cyclic(): lax.ppermute(value, axis, [(source, (source + shift) % count) for source...]
    ppermute x0 -> x12, starting transfers between devices: none -> 18.8 us  [cyclic(): lax.ppermute(value, axis, [(source, (source + shift) % count) for source...]
    psum x3 -> x1, blocking collectives: 25.1 us -> 9.76 us  [on_device(): sums = lax.psum(sums, 'sector')]
    convert_element_type x4 -> x0, other arithmetic: 9.54 us -> none  [the longest x3 8.68 us: on_device(): state_b = state.astype(bf16)]
  transfers between devices with their start and end apart: 5 -> 16, of which waited for: 5 -> 5; matrix products, arithmetic and copies ran while one was open for 5% -> 3% of each run, Pallas kernels for 0% -> 28%
where the time goes in v2:
time: 164 us; the launch traced here: 162 us
  starting transfers between devices  52.4 us (32%)
  Pallas kernels  51.6 us (31%)
  waiting for transfers between devices  36.6 us (22%)
  blocking collectives  9.76 us (6%)
  local copies, waits for them, and re-layouts  9.36 us (6%)
    pallas_call x11, Pallas kernels, run_kernel(): pl.pallas_call(body, grid=grid, in_specs=in_specs, out_specs=out_specs, o...  51.6 us
    ppermute x4, starting transfers between devices, from_behind(): lax.ppermute(value, axis, [(source, source + steps) for source in range(i...  33.6 us
    ppermute x12, waiting for transfers between devices, cyclic(): lax.ppermute(value, axis, [(source, (source + shift) % count) for source...  23.4 us
    ppermute x12, starting transfers between devices, cyclic(): lax.ppermute(value, axis, [(source, (source + shift) % count) for source...  18.8 us
    ppermute x4, waiting for transfers between devices, from_behind(): lax.ppermute(value, axis, [(source, source + steps) for source in range(i...  13.2 us
    psum x1, blocking collectives, on_device(): sums = lax.psum(sums, 'sector')  9.76 us
    while x33, local copies, waits for them, and re-layouts  6.41 us
  transfers between devices with their start and end apart: 16, of which 5 were waited for; matrix products, arithmetic and copies ran while one was open for 3% of the time, Pallas kernels for 28%

profile of v2, /device:TPU:1, one launch (start us, length us, event | category | flops | bytes accessed | tf_op | source)
XLA Modules:
  0.0 161.5 jit_solution(15168765851486836732)
XLA Ops:
  0.6 4.5 %collective-permute-start.35 = (bf16[2,4,256,256]{3,2,1,0:T(8,128)(2,1)}, bf16[2,4,256,256]{3,2,1,0:T(8,128)(2,1)}, u32[]{:S(2)}, u32[]{:S(2)}) collective-permute-start(bf16[2,4,256,256]{3,2,1,0:T(8,128)(2,1)} %bitcast.42), channel_id=1, source_target_pairs={{0,4},{4,8},{8,12},{12,16},{16,20},{20,24},{24,28},{1,5},{5,9},{9,... | collective-permute-start | bytes 3145736 | tf_op jit(solution)/shard_map/ppermute | solution.py:35
  5.1 1.9 %collective-permute-start.36 = (bf16[2,4,256,256]{3,2,1,0:T(8,128)(2,1)}, bf16[2,4,256,256]{3,2,1,0:T(8,128)(2,1)}, u32[]{:S(2)}, u32[]{:S(2)}) collective-permute-start(bf16[2,4,256,256]{3,2,1,0:T(8,128)(2,1)} %bitcast.54), channel_id=1, source_target_pairs={{4,0},{8,4},{12,8},{16,12},{20,16},{24,20},{28,24},{5,1},{9,5},{13... | collective-permute-start | bytes 3145736 | tf_op jit(solution)/shard_map/ppermute | solution.py:35
  7.1 1.3 collective-permute-start.30
  8.4 2.3 %collective-permute-start.31 = (s32[4]{0:T(128)}, s32[4]{0:T(128)S(1)}, u32[]{:S(2)}, u32[]{:S(2)}) collective-permute-start(s32[4]{0:T(128)} %bitcast.88), channel_id=1, source_target_pairs={{0,2},{1,3},{2,0},{3,1},{4,6},{5,7},{6,4},{7,5},{8,10},{9,11},{10,... | collective-permute-start | bytes 56 | tf_op jit(solution)/shard_map/ppermute | solution.py:40
  10.7 1.1 collective-permute-start.32
  11.8 2.3 %shard_map.104 = (f32[4,256,256]{2,1,0:T(8,128)S(1)}, bf16[2048,128]{1,0:T(8,128)(2,1)S(1)}) custom-call(s32[4]{0:T(128)} %bitcast.90, f32[4,256,256]{2,1,0:T(8,128)} %bitcast.86), custom_call_target="tpu_custom_call" | custom-call | bytes 2621456 | tf_op jit(solution)/shard_map/pallas_call | solution.py:380
  14.1 0.0 collective-permute-done.30.refs_1_
  14.1 0.0 copy-start.69
  14.1 0.0 copy-start.70
  14.2 0.0 collective-permute-done.32.refs_3_
  14.2 0.5 copy-done.69
  14.6 0.0 copy-done.70
  14.7 0.1 copy-done.71
  14.8 1.5 shard_map.103
  16.9 84.1 %conditional.1 = (f32[4,256,256]{2,1,0:T(8,128)S(1)}, f32[4,256,256]{2,1,0:T(8,128)}, f32[8,128]{1,0:T(8,128)}) conditional(s32[]{:T(128)} %bitcast.12, (s32[41]{0:T(128)}, bf16[2048,128]{1,0:T(8,128)(2,1)S(1)}, bf16[2,4,256,256]{3,2,1,0:T(8,128)(2,1)}, bf16[2,4,256,256]{3,2,1,0:T(8,128)(2,1)}, f32[1,3]{1,0:T(1,128)}, ...), branch_computations={%region_0.0_spmd, %region_3.0_spmd, %region_6.0_spmd, %region_9.0_... | conditional | flops 1073741824 | bytes 40494176 | solution.py:498
  17.0 0.0 copy-start.1
  17.0 0.0 copy-start.57
  17.0 2.0 %branch_0_fun.1 = (bf16[1024,128]{1,0:T(8,128)(2,1)}, bf16[704,128]{1,0:T(8,128)(2,1)S(1)}, bf16[1024,128]{1,0:T(8,128)(2,1)}) custom-call(s32[41]{0:T(128)} %get-tuple-element.4254.table_ref, bf16[2048,128]{1,0:T(8,128)(2,1)S(1)} %get-tuple-element.4250.own_ref), custom_call_target="tpu_custom_call" | custom-call | bytes 1228964 | tf_op jit(solution)/shard_map/cond/branch_0_fun/pallas_call | solution.py:380
  19.0 1.0 copy.289
  20.0 0.6 broadcast.20
  20.6 80.2 %while.240 = (s32[]{:T(128)}, f32[4,256,256]{2,1,0:T(8,128)S(1)}, f32[4,256,256]{2,1,0:T(8,128)}, f32[8,128]{1,0:T(8,128)}, bf16[2048,128]{1,0:T(8,128)(2,1)S(1)...) while((s32[]{:T(128)}, f32[4,256,256]{2,1,0:T(8,128)S(1)}, ...), condition=%wide.region_2.0_spmd, body=%wide.region_1.0_spmd.sunk | while | flops 1073741824 | bytes 27509488 | solution.py:495
  20.6 0.4 collective-permute-start.27
  21.0 2.9 %collective-permute-start.29 = (bf16[1024,128]{1,0:T(8,128)(2,1)}, bf16[1024,128]{1,0:T(8,128)(2,1)S(1)}, u32[]{:S(2)}, u32[]{:S(2)}) collective-permute-start(bf16[1024,128]{1,0:T(8,128)(2,1)} %get-tuple-element.4268), channel_id=1, source_target_pairs={{0,3},{1,0},{2,1},{3,2},{4,7},{5,4},{6,5},{7,6},{8,11},{9,8},{10,9... | collective-permute-start | bytes 786440 | tf_op jit(solution)/shard_map/cond/branch_0_fun/while/body/eval_jaxpr/ppermute | solution.py:40
  23.8 0.0 collective-permute-start.28
  23.8 1.3 copy.380.sums_ref
  25.1 4.7 %eval_jaxpr.78.refs_6_ = f32[4,256,256]{2,1,0:T(8,128)} custom-call(s32[41]{0:T(128)} %get-tuple-element.4284.table_ref, bf16[2048,128]{1,0:T(8,128)(2,1)S(1)} %get-tuple-element.4265.own_ref.refs_0_, bf16[2,4,256,256]{3,2,1,0:T(8,128)(2,1)S(1)} %get-tuple-element.4285.left_ref, bf16[2,4,256,256]{3,2,1,0:T(8,128)(2,1)} %get-tuple-element.4286.right_ref), custom_call_target="tpu_custom_call" | custom-call | flops 536870912 | bytes 3670180 | tf_op jit(solution)/shard_map/cond/branch_0_fun/while/body/eval_jaxpr/pallas_call | solution.py:380
  29.8 16.0 %collective-permute-done.28.refs_2_ = bf16[704,128]{1,0:T(8,128)(2,1)S(1)} collective-permute-done((bf16[704,128]{1,0:T(8,128)(2,1)S(1)}, bf16[704,128]{1,0:T(8,128)(2,1)S(1)}, u32[]{:S(2)}, u32[]{:S(2)}) %collective-permute-start.28) | collective-permute-done | bytes 180256 | tf_op jit(solution)/shard_map/cond/branch_0_fun/while/body/eval_jaxpr/ppermute | solution.py:40
  45.8 0.0 collective-permute-done.27.refs_1_
  45.8 0.0 collective-permute-done.29.refs_3_
  45.8 0.7 copy-done.55
  46.5 0.1 copy-done.49
  46.6 0.1 copy-done.50
  46.7 7.4 %eval_jaxpr.79 = (f32[4,256,256]{2,1,0:T(8,128)S(1)}, f32[4,256,256]{2,1,0:T(8,128)}, f32[8,128]{1,0:T(8,128)}, bf16[2048,128]{1,0:T(8,128)(2,1)S(1)}, bf16[1024...) custom-call(s32[41]{0:T(128)} %get-tuple-element.4284.table_ref, ...), custom_call_target="tpu_custom_call", output_to_operand_aliasing={{3}: (4, {}), {0}: (11, {}), {1}: (12, {})} | custom-call | flops 536870912 | bytes 9806004 | tf_op jit(solution)/shard_map/cond/branch_0_fun/while/body/eval_jaxpr/pallas_call | solution.py:380
  54.1 0.1 collective-permute-start.27
  54.2 3.3 %collective-permute-start.29 = (bf16[1024,128]{1,0:T(8,128)(2,1)}, bf16[1024,128]{1,0:T(8,128)(2,1)S(1)}, u32[]{:S(2)}, u32[]{:S(2)}) collective-permute-start(bf16[1024,128]{1,0:T(8,128)(2,1)} %get-tuple-element.4268), channel_id=1, source_target_pairs={{0,3},{1,0},{2,1},{3,2},{4,7},{5,4},{6,5},{7,6},{8,11},{9,8},{10,9... | collective-permute-start | bytes 786440 | tf_op jit(solution)/shard_map/cond/branch_0_fun/while/body/eval_jaxpr/ppermute | solution.py:40
  57.4 0.0 collective-permute-start.28
  57.4 1.3 copy.380.sums_ref
  58.7 4.7 %eval_jaxpr.78.refs_6_ = f32[4,256,256]{2,1,0:T(8,128)} custom-call(s32[41]{0:T(128)} %get-tuple-element.4284.table_ref, bf16[2048,128]{1,0:T(8,128)(2,1)S(1)} %get-tuple-element.4265.own_ref.refs_0_, bf16[2,4,256,256]{3,2,1,0:T(8,128)(2,1)S(1)} %get-tuple-element.4285.left_ref, bf16[2,4,256,256]{3,2,1,0:T(8,128)(2,1)} %get-tuple-element.4286.right_ref), custom_call_target="tpu_custom_call" | custom-call | flops 536870912 | bytes 3670180 | tf_op jit(solution)/shard_map/cond/branch_0_fun/while/body/eval_jaxpr/pallas_call | solution.py:380
  63.4 4.0 %collective-permute-done.28.refs_2_ = bf16[704,128]{1,0:T(8,128)(2,1)S(1)} collective-permute-done((bf16[704,128]{1,0:T(8,128)(2,1)S(1)}, bf16[704,128]{1,0:T(8,128)(2,1)S(1)}, u32[]{:S(2)}, u32[]{:S(2)}) %collective-permute-start.28) | collective-permute-done | bytes 180256 | tf_op jit(solution)/shard_map/cond/branch_0_fun/while/body/eval_jaxpr/ppermute | solution.py:40
  67.3 0.0 collective-permute-done.27.refs_1_
  67.3 0.0 collective-permute-done.29.refs_3_
  67.4 0.7 copy-done.55
  68.0 0.1 copy-done.49
  68.1 0.1 copy-done.50
  68.2 7.4 %eval_jaxpr.79 = (f32[4,256,256]{2,1,0:T(8,128)S(1)}, f32[4,256,256]{2,1,0:T(8,128)}, f32[8,128]{1,0:T(8,128)}, bf16[2048,128]{1,0:T(8,128)(2,1)S(1)}, bf16[1024...) custom-call(s32[41]{0:T(128)} %get-tuple-element.4284.table_ref, ...), custom_call_target="tpu_custom_call", output_to_operand_aliasing={{3}: (4, {}), {0}: (11, {}), {1}: (12, {})} | custom-call | flops 536870912 | bytes 9806004 | tf_op jit(solution)/shard_map/cond/branch_0_fun/while/body/eval_jaxpr/pallas_call | solution.py:380
  75.7 6.3 %collective-permute-start.27 = (bf16[1024,128]{1,0:T(8,128)(2,1)}, bf16[1024,128]{1,0:T(8,128)(2,1)S(1)}, u32[]{:S(2)}, u32[]{:S(2)}) collective-permute-start(bf16[1024,128]{1,0:T(8,128)(2,1)} %get-tuple-element.4266), channel_id=1, source_target_pairs={{0,1},{1,2},{2,3},{3,0},{4,5},{5,6},{6,7},{7,4},{8,9},{9,10},{10,1... | collective-permute-start | bytes 786440 | tf_op jit(solution)/shard_map/cond/branch_0_fun/while/body/eval_jaxpr/ppermute | solution.py:40
  81.9 1.2 collective-permute-start.28
  83.2 1.3 copy.380.sums_ref
  84.4 4.7 %eval_jaxpr.78.refs_6_ = f32[4,256,256]{2,1,0:T(8,128)} custom-call(s32[41]{0:T(128)} %get-tuple-element.4284.table_ref, bf16[2048,128]{1,0:T(8,128)(2,1)S(1)} %get-tuple-element.4265.own_ref.refs_0_, bf16[2,4,256,256]{3,2,1,0:T(8,128)(2,1)S(1)} %get-tuple-element.4285.left_ref, bf16[2,4,256,256]{3,2,1,0:T(8,128)(2,1)} %get-tuple-element.4286.right_ref), custom_call_target="tpu_custom_call" | custom-call | flops 536870912 | bytes 3670180 | tf_op jit(solution)/shard_map/cond/branch_0_fun/while/body/eval_jaxpr/pallas_call | solution.py:380
  89.1 3.4 %collective-permute-done.28.refs_2_ = bf16[704,128]{1,0:T(8,128)(2,1)S(1)} collective-permute-done((bf16[704,128]{1,0:T(8,128)(2,1)S(1)}, bf16[704,128]{1,0:T(8,128)(2,1)S(1)}, u32[]{:S(2)}, u32[]{:S(2)}) %collective-permute-start.28) | collective-permute-done | bytes 180256 | tf_op jit(solution)/shard_map/cond/branch_0_fun/while/body/eval_jaxpr/ppermute | solution.py:40
  92.5 0.0 collective-permute-done.27.refs_1_
  92.5 0.7 copy-done.55
  93.1 0.1 copy-done.49
  93.2 0.1 copy-done.50
  93.4 7.4 %eval_jaxpr.79 = (f32[4,256,256]{2,1,0:T(8,128)S(1)}, f32[4,256,256]{2,1,0:T(8,128)}, f32[8,128]{1,0:T(8,128)}, bf16[2048,128]{1,0:T(8,128)(2,1)S(1)}, bf16[1024...) custom-call(s32[41]{0:T(128)} %get-tuple-element.4284.table_ref, ...), custom_call_target="tpu_custom_call", output_to_operand_aliasing={{3}: (4, {}), {0}: (11, {}), {1}: (12, {})} | custom-call | flops 536870912 | bytes 9806004 | tf_op jit(solution)/shard_map/cond/branch_0_fun/while/body/eval_jaxpr/pallas_call | solution.py:380
  101.1 0.0 copy-start
  101.1 9.8 %psum.7.sums_ref = f32[8,128]{1,0:T(8,128)} all-reduce(f32[8,128]{1,0:T(8,128)} %get-tuple-element.2564), channel_id=1, replica_groups=mesh['chain'=8,'sector'=4] {'sector'}, use_global_device_ids=true, to_apply=%region_30.0 | all-reduce | flops 1024 | bytes 8192 | tf_op jit(solution)/shard_map/psum | solution.py:503
  110.8 3.9 %shard_map.105 = (f32[4,256,256]{2,1,0:T(8,128)}, bf16[4,256,256]{2,1,0:T(8,128)(2,1)}) custom-call(f32[1,3]{1,0:T(1,128)} %step_ref.1, f32[8,128]{1,0:T(8,128)} %psum.7.sums_ref, f32[4,256,256]{2,1,0:T(8,128)S(1)} %get-tuple-element.2565.state_ref, f32[4,256,256]{2,1,0:T(8,128)} %get-tuple-element.2566.image_ref), custom_call_target="tpu_custom_call" | custom-call | bytes 3674124 | tf_op jit(solution)/shard_map/pallas_call | solution.py:380
  114.7 25.2 %collective-permute-start.33 = (bf16[4,256,256]{2,1,0:T(8,128)(2,1)}, bf16[4,256,256]{2,1,0:T(8,128)(2,1)S(1)}, u32[]{:S(2)}, u32[]{:S(2)}) collective-permute-start(bf16[4,256,256]{2,1,0:T(8,128)(2,1)} %get-tuple-element.2568), channel_id=1, source_target_pairs={{0,4},{4,8},{8,12},{12,16},{16,20},{20,24},{24,28},{1,5},{5,9},{9,... | collective-permute-start | bytes 1572872 | tf_op jit(solution)/shard_map/ppermute | solution.py:35
  140.0 1.9 %collective-permute-start.34 = (bf16[4,256,256]{2,1,0:T(8,128)(2,1)}, bf16[4,256,256]{2,1,0:T(8,128)(2,1)S(1)}, u32[]{:S(2)}, u32[]{:S(2)}) collective-permute-start(bf16[4,256,256]{2,1,0:T(8,128)(2,1)} %get-tuple-element.2568), channel_id=1, source_target_pairs={{4,0},{8,4},{12,8},{16,12},{20,16},{24,20},{28,24},{5,1},{9,5},{13... | collective-permute-start | bytes 1572872 | tf_op jit(solution)/shard_map/ppermute | solution.py:35
  141.9 4.5 %collective-permute-done.33.from_left = bf16[4,256,256]{2,1,0:T(8,128)(2,1)S(1)} collective-permute-done((bf16[4,256,256]{2,1,0:T(8,128)(2,1)}, bf16[4,256,256]{2,1,0:T(8,128)(2,1)S(1)}, u32[]{:S(2)}, u32[]{:S(2)}) %collective-permute-start.33) | collective-permute-done | bytes 524320 | tf_op jit(solution)/shard_map/ppermute | solution.py:35
  146.4 8.7 %collective-permute-done.34.from_right = bf16[4,256,256]{2,1,0:T(8,128)(2,1)S(1)} collective-permute-done((bf16[4,256,256]{2,1,0:T(8,128)(2,1)}, bf16[4,256,256]{2,1,0:T(8,128)(2,1)S(1)}, u32[]{:S(2)}, u32[]{:S(2)}) %collective-permute-start.34) | collective-permute-done | bytes 524320 | tf_op jit(solution)/shard_map/ppermute | solution.py:35
  155.1 0.8 copy-done.68
  155.8 5.7 %shard_map.106 = (f32[2,4,256,256]{3,2,1,0:T(8,128)}, f32[2,4,256,256]{3,2,1,0:T(8,128)}) custom-call(bf16[4,256,256]{2,1,0:T(8,128)(2,1)} %copy-done.67, bf16[4,256,256]{2,1,0:T(8,128)(2,1)} %copy-done.68, bf16[2,4,256,256]{3,2,1,0:T(8,128)(2,1)} %collective-permute-done.35.left_next, bf16[2,4,256,256]{3,2,1,0:T(8,128)(2,1)} %collective-permute-done.36.right_next, ...), custom_call_target="tpu_custom_call" | custom-call | flops 1073741824 | bytes 9437184 | tf_op jit(solution)/shard_map/pallas_call | solution.py:380
  (35 shorter events, 0.1 us)
Async XLA Ops:
  0.6 154.4 %collective-permute-start.35 = (bf16[2,4,256,256]{3,2,1,0:T(8,128)(2,1)}, bf16[2,4,256,256]{3,2,1,0:T(8,128)(2,1)}, u32[]{:S(2)}, u32[]{:S(2)}) collective-permute-start(bf16[2,4,256,256]{3,2,1,0:T(8,128)(2,1)} %bitcast.42), channel_id=1, source_target_pairs={{0,4},{4,8},{8,12},{12,16},{16,20},{20,24},{24,28},{1,5},{5,9},{9,... | collective-permute-start | bytes 3145736 | tf_op jit(solution)/shard_map/ppermute | solution.py:35
  5.1 149.9 %collective-permute-start.36 = (bf16[2,4,256,256]{3,2,1,0:T(8,128)(2,1)}, bf16[2,4,256,256]{3,2,1,0:T(8,128)(2,1)}, u32[]{:S(2)}, u32[]{:S(2)}) collective-permute-start(bf16[2,4,256,256]{3,2,1,0:T(8,128)(2,1)} %bitcast.54), channel_id=1, source_target_pairs={{4,0},{8,4},{12,8},{16,12},{20,16},{24,20},{28,24},{5,1},{9,5},{13... | collective-permute-start | bytes 3145736 | tf_op jit(solution)/shard_map/ppermute | solution.py:35
  7.1 7.0 %collective-permute-start.30 = (s32[4]{0:T(128)}, s32[4]{0:T(128)S(1)}, u32[]{:S(2)}, u32[]{:S(2)}) collective-permute-start(s32[4]{0:T(128)} %bitcast.87), channel_id=1, source_target_pairs={{0,1},{1,2},{2,3},{3,0},{4,5},{5,6},{6,7},{7,4},{8,9},{9,10},{10,1... | collective-permute-start | bytes 56 | tf_op jit(solution)/shard_map/ppermute | solution.py:40
  8.4 5.7 %collective-permute-start.31 = (s32[4]{0:T(128)}, s32[4]{0:T(128)S(1)}, u32[]{:S(2)}, u32[]{:S(2)}) collective-permute-start(s32[4]{0:T(128)} %bitcast.88), channel_id=1, source_target_pairs={{0,2},{1,3},{2,0},{3,1},{4,6},{5,7},{6,4},{7,5},{8,10},{9,11},{10,... | collective-permute-start | bytes 56 | tf_op jit(solution)/shard_map/ppermute | solution.py:40
  10.7 3.4 %collective-permute-start.32 = (s32[4]{0:T(128)}, s32[4]{0:T(128)S(1)}, u32[]{:S(2)}, u32[]{:S(2)}) collective-permute-start(s32[4]{0:T(128)} %bitcast.89), channel_id=1, source_target_pairs={{0,3},{1,0},{2,1},{3,2},{4,7},{5,4},{6,5},{7,6},{8,11},{9,8},{10,9... | collective-permute-start | bytes 56 | tf_op jit(solution)/shard_map/ppermute | solution.py:40
  14.1 0.5 copy-start.69
  14.1 0.5 copy-start.70
  14.2 0.6 copy-start.71
  17.0 3.6 %copy-start.1 = (bf16[2,4,256,256]{3,2,1,0:T(8,128)(2,1)S(1)}, bf16[2,4,256,256]{3,2,1,0:T(8,128)(2,1)}, u32[]{:S(2)}) copy-start(bf16[2,4,256,256]{3,2,1,0:T(8,128)(2,1)} %get-tuple-element.4255) | copy-start | bytes 3145732 | tf_op jit(solution)/shard_map/cond
  17.0 3.6 %copy-start.57 = (f32[1,3]{1,0:T(1,128)S(1)}, f32[1,3]{1,0:T(1,128)}, u32[]{:S(2)}) copy-start(f32[1,3]{1,0:T(1,128)} %get-tuple-element.4257) | copy-start | bytes 40 | tf_op jit(solution)/shard_map/cond
  20.6 25.2 %collective-permute-start.27 = (bf16[1024,128]{1,0:T(8,128)(2,1)}, bf16[1024,128]{1,0:T(8,128)(2,1)S(1)}, u32[]{:S(2)}, u32[]{:S(2)}) collective-permute-start(bf16[1024,128]{1,0:T(8,128)(2,1)} %get-tuple-element.4266), channel_id=1, source_target_pairs={{0,1},{1,2},{2,3},{3,0},{4,5},{5,6},{6,7},{7,4},{8,9},{9,10},{10,1... | collective-permute-start | bytes 786440 | tf_op jit(solution)/shard_map/cond/branch_0_fun/while/body/eval_jaxpr/ppermute | solution.py:40
  21.0 24.8 %collective-permute-start.29 = (bf16[1024,128]{1,0:T(8,128)(2,1)}, bf16[1024,128]{1,0:T(8,128)(2,1)S(1)}, u32[]{:S(2)}, u32[]{:S(2)}) collective-permute-start(bf16[1024,128]{1,0:T(8,128)(2,1)} %get-tuple-element.4268), channel_id=1, source_target_pairs={{0,3},{1,0},{2,1},{3,2},{4,7},{5,4},{6,5},{7,6},{8,11},{9,8},{10,9... | collective-permute-start | bytes 786440 | tf_op jit(solution)/shard_map/cond/branch_0_fun/while/body/eval_jaxpr/ppermute | solution.py:40
  23.8 22.0 %collective-permute-start.28 = (bf16[704,128]{1,0:T(8,128)(2,1)S(1)}, bf16[704,128]{1,0:T(8,128)(2,1)S(1)}, u32[]{:S(2)}, u32[]{:S(2)}) collective-permute-start(bf16[704,128]{1,0:T(8,128)(2,1)S(1)} %get-tuple-element.4267), channel_id=1, source_target_pairs={{0,2},{1,3},{2,0},{3,1},{4,6},{5,7},{6,4},{7,5},{8,10},{9,11},{10,... | collective-permute-start | bytes 540680 | tf_op jit(solution)/shard_map/cond/branch_0_fun/while/body/eval_jaxpr/ppermute | solution.py:40
  25.1 21.6 %copy-start.12 = (bf16[2,4,256,256]{3,2,1,0:T(8,128)(2,1)S(1)}, bf16[2,4,256,256]{3,2,1,0:T(8,128)(2,1)}, u32[]{:S(2)}) copy-start(bf16[2,4,256,256]{3,2,1,0:T(8,128)(2,1)} %get-tuple-element.4288.refs_4_) | copy-start | bytes 3145732 | tf_op jit(solution)/shard_map/cond/branch_0_fun/while
  25.1 21.6 %copy-start.22 = (bf16[2,4,256,256]{3,2,1,0:T(8,128)(2,1)S(1)}, bf16[2,4,256,256]{3,2,1,0:T(8,128)(2,1)}, u32[]{:S(2)}) copy-start(bf16[2,4,256,256]{3,2,1,0:T(8,128)(2,1)} %get-tuple-element.4289.refs_5_) | copy-start | bytes 3145732 | tf_op jit(solution)/shard_map/cond/branch_0_fun/while
  45.8 0.7 copy-start.55
  45.8 0.8 copy-start.49
  45.8 0.9 copy-start.50
  54.1 13.2 %collective-permute-start.27 = (bf16[1024,128]{1,0:T(8,128)(2,1)}, bf16[1024,128]{1,0:T(8,128)(2,1)S(1)}, u32[]{:S(2)}, u32[]{:S(2)}) collective-permute-start(bf16[1024,128]{1,0:T(8,128)(2,1)} %get-tuple-element.4266), channel_id=1, source_target_pairs={{0,1},{1,2},{2,3},{3,0},{4,5},{5,6},{6,7},{7,4},{8,9},{9,10},{10,1... | collective-permute-start | bytes 786440 | tf_op jit(solution)/shard_map/cond/branch_0_fun/while/body/eval_jaxpr/ppermute | solution.py:40
  54.2 13.2 %collective-permute-start.29 = (bf16[1024,128]{1,0:T(8,128)(2,1)}, bf16[1024,128]{1,0:T(8,128)(2,1)S(1)}, u32[]{:S(2)}, u32[]{:S(2)}) collective-permute-start(bf16[1024,128]{1,0:T(8,128)(2,1)} %get-tuple-element.4268), channel_id=1, source_target_pairs={{0,3},{1,0},{2,1},{3,2},{4,7},{5,4},{6,5},{7,6},{8,11},{9,8},{10,9... | collective-permute-start | bytes 786440 | tf_op jit(solution)/shard_map/cond/branch_0_fun/while/body/eval_jaxpr/ppermute | solution.py:40
  57.4 9.9 %collective-permute-start.28 = (bf16[704,128]{1,0:T(8,128)(2,1)S(1)}, bf16[704,128]{1,0:T(8,128)(2,1)S(1)}, u32[]{:S(2)}, u32[]{:S(2)}) collective-permute-start(bf16[704,128]{1,0:T(8,128)(2,1)S(1)} %get-tuple-element.4267), channel_id=1, source_target_pairs={{0,2},{1,3},{2,0},{3,1},{4,6},{5,7},{6,4},{7,5},{8,10},{9,11},{10,... | collective-permute-start | bytes 540680 | tf_op jit(solution)/shard_map/cond/branch_0_fun/while/body/eval_jaxpr/ppermute | solution.py:40
  58.7 9.5 %copy-start.12 = (bf16[2,4,256,256]{3,2,1,0:T(8,128)(2,1)S(1)}, bf16[2,4,256,256]{3,2,1,0:T(8,128)(2,1)}, u32[]{:S(2)}) copy-start(bf16[2,4,256,256]{3,2,1,0:T(8,128)(2,1)} %get-tuple-element.4288.refs_4_) | copy-start | bytes 3145732 | tf_op jit(solution)/shard_map/cond/branch_0_fun/while
  58.7 9.5 %copy-start.22 = (bf16[2,4,256,256]{3,2,1,0:T(8,128)(2,1)S(1)}, bf16[2,4,256,256]{3,2,1,0:T(8,128)(2,1)}, u32[]{:S(2)}) copy-start(bf16[2,4,256,256]{3,2,1,0:T(8,128)(2,1)} %get-tuple-element.4289.refs_5_) | copy-start | bytes 3145732 | tf_op jit(solution)/shard_map/cond/branch_0_fun/while
  67.3 0.7 copy-start.55
  67.3 0.8 copy-start.49
  67.3 0.9 copy-start.50
  75.7 16.8 %collective-permute-start.27 = (bf16[1024,128]{1,0:T(8,128)(2,1)}, bf16[1024,128]{1,0:T(8,128)(2,1)S(1)}, u32[]{:S(2)}, u32[]{:S(2)}) collective-permute-start(bf16[1024,128]{1,0:T(8,128)(2,1)} %get-tuple-element.4266), channel_id=1, source_target_pairs={{0,1},{1,2},{2,3},{3,0},{4,5},{5,6},{6,7},{7,4},{8,9},{9,10},{10,1... | collective-permute-start | bytes 786440 | tf_op jit(solution)/shard_map/cond/branch_0_fun/while/body/eval_jaxpr/ppermute | solution.py:40
  81.9 10.6 %collective-permute-start.29 = (bf16[1024,128]{1,0:T(8,128)(2,1)}, bf16[1024,128]{1,0:T(8,128)(2,1)S(1)}, u32[]{:S(2)}, u32[]{:S(2)}) collective-permute-start(bf16[1024,128]{1,0:T(8,128)(2,1)} %get-tuple-element.4268), channel_id=1, source_target_pairs={{0,3},{1,0},{2,1},{3,2},{4,7},{5,4},{6,5},{7,6},{8,11},{9,8},{10,9... | collective-permute-start | bytes 786440 | tf_op jit(solution)/shard_map/cond/branch_0_fun/while/body/eval_jaxpr/ppermute | solution.py:40
  81.9 10.5 %collective-permute-start.28 = (bf16[704,128]{1,0:T(8,128)(2,1)S(1)}, bf16[704,128]{1,0:T(8,128)(2,1)S(1)}, u32[]{:S(2)}, u32[]{:S(2)}) collective-permute-start(bf16[704,128]{1,0:T(8,128)(2,1)S(1)} %get-tuple-element.4267), channel_id=1, source_target_pairs={{0,2},{1,3},{2,0},{3,1},{4,6},{5,7},{6,4},{7,5},{8,10},{9,11},{10,... | collective-permute-start | bytes 540680 | tf_op jit(solution)/shard_map/cond/branch_0_fun/while/body/eval_jaxpr/ppermute | solution.py:40
  84.4 8.9 %copy-start.12 = (bf16[2,4,256,256]{3,2,1,0:T(8,128)(2,1)S(1)}, bf16[2,4,256,256]{3,2,1,0:T(8,128)(2,1)}, u32[]{:S(2)}) copy-start(bf16[2,4,256,256]{3,2,1,0:T(8,128)(2,1)} %get-tuple-element.4288.refs_4_) | copy-start | bytes 3145732 | tf_op jit(solution)/shard_map/cond/branch_0_fun/while
  84.4 8.9 %copy-start.22 = (bf16[2,4,256,256]{3,2,1,0:T(8,128)(2,1)S(1)}, bf16[2,4,256,256]{3,2,1,0:T(8,128)(2,1)}, u32[]{:S(2)}) copy-start(bf16[2,4,256,256]{3,2,1,0:T(8,128)(2,1)} %get-tuple-element.4289.refs_5_) | copy-start | bytes 3145732 | tf_op jit(solution)/shard_map/cond/branch_0_fun/while
  92.5 0.7 copy-start.55
  92.5 0.8 copy-start.49
  92.5 0.9 copy-start.50
  101.1 54.8 %copy-start = (bf16[1,2,4,256,256]{4,3,2,1,0:T(8,128)(2,1)S(1)}, bf16[1,2,4,256,256]{4,3,2,1,0:T(8,128)(2,1)}, u32[]{:S(2)}) copy-start(bf16[1,2,4,256,256]{4,3,2,1,0:T(8,128)(2,1)} %param.41) | copy-start | bytes 3145732
  110.8 45.0 %copy-start.11 = (bf16[1,2,4,256,256]{4,3,2,1,0:T(8,128)(2,1)S(1)}, bf16[1,2,4,256,256]{4,3,2,1,0:T(8,128)(2,1)}, u32[]{:S(2)}) copy-start(bf16[1,2,4,256,256]{4,3,2,1,0:T(8,128)(2,1)} %param.42) | copy-start | bytes 3145732
  114.7 31.6 %collective-permute-start.33 = (bf16[4,256,256]{2,1,0:T(8,128)(2,1)}, bf16[4,256,256]{2,1,0:T(8,128)(2,1)S(1)}, u32[]{:S(2)}, u32[]{:S(2)}) collective-permute-start(bf16[4,256,256]{2,1,0:T(8,128)(2,1)} %get-tuple-element.2568), channel_id=1, source_target_pairs={{0,4},{4,8},{8,12},{12,16},{16,20},{20,24},{24,28},{1,5},{5,9},{9,... | collective-permute-start | bytes 1572872 | tf_op jit(solution)/shard_map/ppermute | solution.py:35
  140.0 15.1 %collective-permute-start.34 = (bf16[4,256,256]{2,1,0:T(8,128)(2,1)}, bf16[4,256,256]{2,1,0:T(8,128)(2,1)S(1)}, u32[]{:S(2)}, u32[]{:S(2)}) collective-permute-start(bf16[4,256,256]{2,1,0:T(8,128)(2,1)} %get-tuple-element.2568), channel_id=1, source_target_pairs={{4,0},{8,4},{12,8},{16,12},{20,16},{24,20},{28,24},{5,1},{9,5},{13... | collective-permute-start | bytes 1572872 | tf_op jit(solution)/shard_map/ppermute | solution.py:35
  146.4 8.7 %copy-start.67 = (bf16[4,256,256]{2,1,0:T(8,128)(2,1)}, bf16[4,256,256]{2,1,0:T(8,128)(2,1)S(1)}, u32[]{:S(2)}) copy-start(bf16[4,256,256]{2,1,0:T(8,128)(2,1)S(1)} %collective-permute-done.33.from_left) | copy-start | bytes 1572868
  155.0 0.8 copy-start.68
